TPU v7x, 32 devices: a whole 2x2x4 slice. The times are simulated.
32 devices in a mesh: img: 8 (over z, y), tile: 4 (over x, core).
Axes of the slice: x: 2, y: 2, z: 4, core: 2. Of those that a mesh axis runs over, the one named last changes fastest.
Arguments:
- patches: bfloat16 [8, 1024, 768], P('img', 'tile'), may hold values from -6 to 6
- labels: int32 [8, 1024, 256], P('img', 'tile'), may hold values from 0 to 149
- heights: int32 [8], P('img'), may hold values from 49 to 64, as said below
- cls_emb: bfloat16 [150, 768], P(None, 'img'), may hold values from -6 to 6
- gain_one: bfloat16 [768], P('img'), may hold values from 0.099609375 to 1.8984375
- w_qkv: bfloat16 [768, 2304], P('img'), may hold values from -0.21875 to 0.21875
- w_out: bfloat16 [768, 768], P('img'), may hold values from -6 to 6
- gain_two: bfloat16 [768], P('img'), may hold values from 0.099609375 to 1.8984375
- w_in: bfloat16 [768, 3072], P('img'), may hold values from -0.21875 to 0.21875
- w_back: bfloat16 [3072, 768], P('img'), may hold values from -0.109375 to 0.109375
- head_gain: bfloat16 [150], replicated, may hold values from 1.5 to 4
Outputs:
- masks: bfloat16 [8, 150, 1024, 256], P('img', None, 'tile')
- patch_grad: float32 [8, 1024, 768], P('img', 'tile')
- cls_grad: float32 [150, 768], P(None, 'img')
- gain_one_grad: float32 [768], P('img')
- w_qkv_grad: float32 [768, 2304], P('img')
- w_out_grad: float32 [768, 768], P('img')
- gain_two_grad: float32 [768], P('img')
- w_in_grad: float32 [768, 3072], P('img')
- w_back_grad: float32 [3072, 768], P('img')
- head_gain_grad: float32 [150], replicated
Inputs may be any that keep to these rules, and one draw needn't show every extreme that they name: `heights`: every image has more than 48 patch rows; in every draw some image has all 64.
All inputs are finite; a program needn't handle non-finite values.
Results may differ from a plain program's by a relative error of at most 0.018.
Values may be sent and summed in bfloat16 or wider, within the bound.
A program may use at most 192 MiB of HBM per device.

v0:
```python
import jax
import jax.numpy as jnp
from jax import lax
from jax.sharding import PartitionSpec as P

HEADS = 12
WP = 16
UP = 16


def padded_2(x, sides, width):
    for axis, dim in sides:
        devices, length = (lax.axis_size(axis), x.shape[dim])
        up = [(i, (i + 1) % devices) for i in range(devices - 1)]
        down = [(j, i) for i, j in up]
        last = lax.slice_in_dim(x, length - width, length, axis=dim)
        initial = lax.slice_in_dim(x, 0, width, axis=dim)
        before = lax.ppermute(last, axis, up)
        after = lax.ppermute(initial, axis, down)
        x = jnp.concatenate([before, x, after], axis=dim)
    return x


def product(left, right):
    return jnp.dot(left, right, preferred_element_type=jnp.float32)


def times_transposed(left, right):
    return lax.dot_general(
        left, right, (((1,), (1,)), ((), ())), preferred_element_type=jnp.float32
    )


def transposed_times(left, right):
    return lax.dot_general(
        left, right, (((0,), (0,)), ((), ())), preferred_element_type=jnp.float32
    )


def layer_norm(value, gain):
    centre = jnp.mean(value, axis=-1, keepdims=True)
    centred = value - centre
    spread = jnp.mean(centred * centred, axis=-1, keepdims=True)
    return centred * lax.rsqrt(spread + 1e-05) * gain


def unit_rows(value):
    return value * lax.rsqrt(jnp.sum(value * value, axis=-1, keepdims=True) + 1e-06)


def tent_table(pixel_first, pixels, cell_first, cells, total_cells):
    place = ((pixel_first + jnp.arange(pixels)).astype(jnp.float32) + 0.5) / UP - 0.5
    place = jnp.clip(place, 0.0, total_cells - 1.0)
    grid_cells = (cell_first + jnp.arange(cells)).astype(jnp.float32)
    return jnp.maximum(0.0, 1.0 - jnp.abs(place[:, None] - grid_cells[None, :]))


def forward_block(tokens, weights, key_valid):
    w_joint, w_project, w_expand, w_reduce, gain_first, gain_second = weights
    row_count, features = tokens.shape
    head_size = features // HEADS
    h_one = layer_norm(tokens, gain_first).astype(jnp.bfloat16)
    joint = product(h_one, w_joint).astype(jnp.bfloat16)
    pairs = lax.all_gather(joint[:, features:], "tile", axis=0, tiled=True)
    queries = joint[:, :features].reshape(row_count, HEADS, head_size)
    keys_all = pairs[:, :features].reshape(-1, HEADS, head_size)
    values_all = pairs[:, features:].reshape(-1, HEADS, head_size)
    scores = jnp.einsum(
        "qhd,khd->hqk", queries, keys_all, preferred_element_type=jnp.float32
    ) * head_size ** (-0.5)
    scores = jnp.where(key_valid[None, None, :], scores, -1e30)
    largest = jnp.max(scores, axis=-1, keepdims=True)
    powers = jnp.exp(scores - largest)
    probability = powers / jnp.sum(powers, axis=-1, keepdims=True)
    prob_low = probability.astype(jnp.bfloat16)
    mixed = jnp.einsum("hqk,khd->qhd", prob_low, values_all, preferred_element_type=jnp.float32)
    mixed = mixed.reshape(row_count, features).astype(jnp.bfloat16)
    after_attn = tokens + product(mixed, w_project)
    h_two = layer_norm(after_attn, gain_second).astype(jnp.bfloat16)
    pre_act = product(h_two, w_expand)
    activation = jax.nn.gelu(pre_act).astype(jnp.bfloat16)
    final_rows = after_attn + product(activation, w_reduce)
    stored = (
        h_one,
        queries,
        keys_all,
        values_all,
        probability,
        prob_low,
        mixed,
        after_attn,
        h_two,
        pre_act,
        activation,
    )
    return (final_rows, stored)


def shards(
    patches, labels, heights, cls_emb, gain_one, w_qkv, w_out, gain_two, w_in, w_back, head_gain
):
    tile_index = lax.axis_index("tile")
    tile_count = lax.axis_size("tile")
    own_rows = patches.shape[1]
    grid_rows = own_rows // WP
    classes = head_gain.shape[0]
    per_tile = -(-classes // tile_count)
    padded = per_tile * tile_count
    gathered = (
        lax.all_gather(w_qkv, "img", axis=0, tiled=True),
        lax.all_gather(w_out, "img", axis=0, tiled=True),
        lax.all_gather(w_in, "img", axis=0, tiled=True),
        lax.all_gather(w_back, "img", axis=0, tiled=True),
        lax.all_gather(gain_one, "img", axis=0, tiled=True),
        lax.all_gather(gain_two, "img", axis=0, tiled=True),
        lax.all_gather(cls_emb, "img", axis=1, tiled=True),
    )
    w_joint, w_project, w_expand, w_reduce, gain_first, gain_second, cls_full = gathered
    features = w_project.shape[1]
    head_size = features // HEADS
    gain_first = gain_first.astype(jnp.float32)
    gain_second = gain_second.astype(jnp.float32)
    weights = (w_joint, w_project, w_expand, w_reduce, gain_first, gain_second)
    cls_padded = jnp.pad(cls_full, ((0, padded - classes), (0, 0)))
    cls_rows = lax.dynamic_slice_in_dim(cls_padded, tile_index * per_tile, per_tile, 0)
    tokens = jnp.concatenate([patches[0], cls_rows], axis=0).astype(jnp.float32)
    row_count = own_rows + per_tile
    height = heights[0]
    key_index = jnp.arange(tile_count * row_count)
    key_owner = key_index // row_count
    key_place = key_index % row_count
    key_valid = jnp.where(
        key_place < own_rows,
        key_owner * grid_rows + key_place // WP < height,
        key_owner * per_tile + key_place - own_rows < classes,
    )
    final_rows, stored = forward_block(tokens, weights, key_valid)
    patch_final = final_rows[:own_rows]
    class_final = final_rows[own_rows:]
    patch_unit = unit_rows(patch_final).astype(jnp.bfloat16)
    class_unit = unit_rows(class_final).astype(jnp.bfloat16)
    class_all = lax.all_gather(class_unit, "tile", axis=0, tiled=True)[:classes]
    logits = times_transposed(patch_unit, class_all)
    gain_head = head_gain.astype(jnp.float32)
    normed = layer_norm(logits, gain_head).astype(jnp.bfloat16)
    grid = normed.reshape(grid_rows, WP, classes)
    rimmed = padded_2(grid, (("tile", 0),), 1)
    tile_pixels = grid_rows * UP
    wide_pixels = WP * UP
    down_table = tent_table(
        tile_index * tile_pixels,
        tile_pixels,
        tile_index * grid_rows - 1,
        grid_rows + 2,
        grid_rows * tile_count,
    )
    across_table = tent_table(0, wide_pixels, 0, WP, WP)
    across_low = across_table.astype(jnp.bfloat16)
    widened = jnp.einsum("hwc,qw->hqc", rimmed, across_low, preferred_element_type=jnp.float32)
    band_rows = 32
    band_cells = 4
    pixel_limit = height * UP - tile_index * tile_pixels
    class_ids = jnp.arange(classes)[:, None, None]
    label_grid = labels[0]

    def pixel_band(block_index, carry):
        mask_buffer, grid_sums = carry
        first_row = block_index * band_rows
        first_cell = first_row // UP
        row_band = lax.dynamic_slice(down_table, (first_row, first_cell), (band_rows, band_cells))
        cell_band = lax.dynamic_slice_in_dim(widened, first_cell, band_cells, 0)
        upsampled = jnp.einsum("ph,hqc->cpq", row_band, cell_band, precision=lax.Precision.HIGHEST)
        mask_buffer = lax.dynamic_update_slice_in_dim(
            mask_buffer, upsampled.astype(jnp.bfloat16), first_row, 1
        )
        largest = jnp.max(upsampled, axis=0, keepdims=True)
        powers = jnp.exp(upsampled - largest)
        softmax_value = powers / jnp.sum(powers, axis=0, keepdims=True)
        label_rows = lax.dynamic_slice_in_dim(label_grid, first_row, band_rows, 0)
        target = (label_rows[None] == class_ids).astype(jnp.float32)
        counted = (first_row + jnp.arange(band_rows) < pixel_limit).astype(jnp.float32)[
            None, :, None
        ]
        pixel_grad = (softmax_value - target) * counted / (UP * UP)
        narrowed = jnp.einsum(
            "cpq,qw->cpw", pixel_grad, across_table, precision=lax.Precision.HIGHEST
        )
        cell_grad = jnp.einsum("ph,cpw->hwc", row_band, narrowed, precision=lax.Precision.HIGHEST)
        current = lax.dynamic_slice_in_dim(grid_sums, first_cell, band_cells, 0)
        grid_sums = lax.dynamic_update_slice_in_dim(grid_sums, current + cell_grad, first_cell, 0)
        return (mask_buffer, grid_sums)

    start_masks = jnp.zeros((classes, tile_pixels, wide_pixels), jnp.bfloat16)
    start_sums = jnp.zeros((grid_rows + 2, WP, classes), jnp.float32)
    mask_buffer, rim_grad = lax.fori_loop(
        0, tile_pixels // band_rows, pixel_band, (start_masks, start_sums)
    )
    rim_pair = jnp.stack([rim_grad[0], rim_grad[-1]], axis=0)
    incoming = padded_2(rim_pair, (("tile", 0),), 1)
    grid_grad = rim_grad[1:-1]
    grid_grad = grid_grad.at[0].add(incoming[0])
    grid_grad = grid_grad.at[-1].add(incoming[-1])
    normed_grad = lax.optimization_barrier(
        grid_grad.reshape(own_rows, classes).astype(jnp.bfloat16)
    ).astype(jnp.float32)
    unused, norm_head_back = jax.vjp(layer_norm, logits, gain_head)
    logit_grad, head_grad = norm_head_back(normed_grad)
    head_total = lax.psum(head_grad, ("img", "tile"))
    logit_low = logit_grad.astype(jnp.bfloat16)
    patch_unit_grad = product(logit_low, class_all)
    class_part = transposed_times(logit_low, patch_unit)
    class_part = jnp.pad(class_part, ((0, padded - classes), (0, 0)))
    class_unit_grad = lax.psum_scatter(class_part, "tile", scatter_dimension=0, tiled=True)
    unused, patch_norm_back = jax.vjp(unit_rows, patch_final)
    unused, class_norm_back = jax.vjp(unit_rows, class_final)
    final_grad = jnp.concatenate(
        [patch_norm_back(patch_unit_grad)[0], class_norm_back(class_unit_grad)[0]], axis=0
    )
    (
        h_one,
        queries,
        keys_all,
        values_all,
        probability,
        prob_low,
        mixed,
        after_attn,
        h_two,
        pre_act,
        activation,
    ) = stored
    branch_low = final_grad.astype(jnp.bfloat16)
    w_back_grad = transposed_times(activation, branch_low)
    act_grad = times_transposed(branch_low, w_reduce)
    unused, gelu_back = jax.vjp(jax.nn.gelu, pre_act)
    pre_low = gelu_back(act_grad)[0].astype(jnp.bfloat16)
    w_in_grad = transposed_times(h_two, pre_low)
    h_two_grad = times_transposed(pre_low, w_expand)
    unused, norm_two_back = jax.vjp(layer_norm, after_attn, gain_second)
    after_part, gain_two_grad = norm_two_back(h_two_grad)
    after_grad = final_grad + after_part
    attn_low = after_grad.astype(jnp.bfloat16)
    w_out_grad = transposed_times(mixed, attn_low)
    mixed_low = (
        times_transposed(attn_low, w_project)
        .astype(jnp.bfloat16)
        .reshape(row_count, HEADS, head_size)
    )
    prob_grad = jnp.einsum(
        "qhd,khd->hqk", mixed_low, values_all, preferred_element_type=jnp.float32
    )
    value_grad = jnp.einsum("hqk,qhd->khd", prob_low, mixed_low, preferred_element_type=jnp.float32)
    score_low = (
        probability * (prob_grad - jnp.sum(probability * prob_grad, axis=-1, keepdims=True))
    ).astype(jnp.bfloat16)
    score_scale = head_size ** (-0.5)
    query_grad = (
        jnp.einsum("hqk,khd->qhd", score_low, keys_all, preferred_element_type=jnp.float32)
        * score_scale
    )
    key_grad = (
        jnp.einsum("hqk,qhd->khd", score_low, queries, preferred_element_type=jnp.float32)
        * score_scale
    )
    pair_grad = jnp.concatenate(
        [key_grad.reshape(-1, features), value_grad.reshape(-1, features)], axis=1
    )
    own_pairs = lax.psum_scatter(
        pair_grad.astype(jnp.bfloat16), "tile", scatter_dimension=0, tiled=True
    ).astype(jnp.float32)
    joint_low = jnp.concatenate(
        [query_grad.reshape(row_count, features), own_pairs], axis=1
    ).astype(jnp.bfloat16)
    w_qkv_grad = transposed_times(h_one, joint_low)
    h_one_grad = times_transposed(joint_low, w_joint)
    unused, norm_one_back = jax.vjp(layer_norm, tokens, gain_first)
    token_part, gain_one_grad = norm_one_back(h_one_grad)
    token_grad = after_grad + token_part
    patch_grad = token_grad[:own_rows][None]
    class_rows_grad = lax.dynamic_update_slice_in_dim(
        jnp.zeros((padded, features), jnp.float32), token_grad[own_rows:], tile_index * per_tile, 0
    )[:classes]
    shares = (
        lax.psum_scatter(w_qkv_grad, "img", scatter_dimension=0, tiled=True),
        lax.psum_scatter(w_out_grad, "img", scatter_dimension=0, tiled=True),
        lax.psum_scatter(gain_one_grad, "img", scatter_dimension=0, tiled=True),
        lax.psum_scatter(class_rows_grad, "img", scatter_dimension=1, tiled=True),
        lax.psum_scatter(w_in_grad, "img", scatter_dimension=0, tiled=True),
        lax.psum_scatter(w_back_grad, "img", scatter_dimension=0, tiled=True),
        lax.psum_scatter(gain_two_grad, "img", scatter_dimension=0, tiled=True),
    )
    totals = (
        lax.psum(shares[0].astype(jnp.bfloat16), "tile").astype(jnp.float32),
        lax.psum(shares[1].astype(jnp.bfloat16), "tile").astype(jnp.float32),
        lax.psum(shares[2].astype(jnp.bfloat16), "tile").astype(jnp.float32),
        lax.psum(shares[3].astype(jnp.bfloat16), "tile").astype(jnp.float32),
        lax.psum(shares[4].astype(jnp.bfloat16), "tile").astype(jnp.float32),
        lax.psum(shares[5].astype(jnp.bfloat16), "tile").astype(jnp.float32),
        lax.psum(shares[6].astype(jnp.bfloat16), "tile").astype(jnp.float32),
    )
    return (
        mask_buffer[None],
        patch_grad,
        totals[3],
        totals[2],
        totals[0],
        totals[1],
        totals[6],
        totals[4],
        totals[5],
        head_total,
    )


def solution(mesh):
    in_specs = (
        P("img", "tile", None),
        P("img", "tile", None),
        P("img"),
        P(None, "img"),
        P("img"),
        P("img", None),
        P("img", None),
        P("img"),
        P("img", None),
        P("img", None),
        P(),
    )
    out_specs = (
        P("img", None, "tile", None),
        P("img", "tile", None),
        P(None, "img"),
        P("img"),
        P("img", None),
        P("img", None),
        P("img"),
        P("img", None),
        P("img", None),
        P(),
    )
    return jax.shard_map(shards, mesh=mesh, in_specs=in_specs, out_specs=out_specs, check_vma=False)
```

profile of v0, /device:TPU:0, one launch (start us, length us, event | category | flops | bytes accessed | tf_op | source)
XLA Modules:
  0.0 1372.3 jit_solution(13839345370739874400)
XLA Ops:
  8.0 33.8 %all-gather = bf16[8,96,150]{1,2,0:T(8,128)(2,1)S(1)} all-gather(bf16[1,96,150]{1,2,0:T(8,128)(2,1)} %bitcast.158), channel_id=1, replica_groups=mesh['img'=8,'tile'=4] {'img'}, dimensions={0}, use_global_device_ids=true | all-gather | bytes 259200 | tf_op jit(solution)/shard_map/all_gather | solution.py:116
  45.9 21.8 %all-reduce.10 = (bf16[768]{0:T(1024)(128)(2,1)S(1)}, bf16[768]{0:T(1024)(128)(2,1)S(1)}) all-reduce(bf16[768]{0:T(1024)(128)(2,1)S(1)} %dynamic-update-slice.6, bf16[768]{0:T(1024)(128)(2,1)S(1)} %dynamic-update-slice.7), channel_id=1, replica_groups=mesh['img'=8,'tile'=4] {'img'}, use_global_device_ids=true, to_apply=%add.2 | all-reduce | flops 1536 | bytes 6144
  70.3 10.0 all-gather.9.cloned.1.call-done
  88.0 26.9 %all-gather.17.cloned.1.call-done = bf16[4,294,1536]{2,1,0:T(8,128)(2,1)} async-done(((bf16[1,294,1536]{2,1,0:T(8,128)(2,1)}), bf16[4,294,1536]{2,1,0:T(8,128)(2,1)}) %all-gather.17.cloned.1.call-update) | async-done | bytes 3612688 | tf_op jit(solution)/shard_map/all_gather | solution.py:64
  130.7 9.9 exponential_reduce_fusion
  140.6 9.1 fusion.70
  149.7 8.4 all-gather.11.cloned.1.call-done
  160.5 78.3 %all-gather.13.cloned.1.call-done = bf16[768,3072]{1,0:T(8,128)(2,1)} async-done(((bf16[96,3072]{1,0:T(8,128)(2,1)}), bf16[768,3072]{1,0:T(8,128)(2,1)}) %all-gather.13.cloned.1.call-update) | async-done | bytes 4718608 | tf_op jit(solution)/shard_map/all_gather | solution.py:112
  238.8 5.8 fusion.142
  244.6 74.3 %all-gather.15.cloned.1.call-done = bf16[3072,768]{1,0:T(8,128)(2,1)} async-done(((bf16[384,768]{1,0:T(8,128)(2,1)}), bf16[3072,768]{1,0:T(8,128)(2,1)}) %all-gather.15.cloned.1.call-update) | async-done | bytes 4718608 | tf_op jit(solution)/shard_map/all_gather | solution.py:113
  318.9 5.7 convolution_add_fusion
  325.0 5.7 all-gather.2
  341.1 7.0 broadcast_in_dim.50
  348.0 188.9 %while.20 = (s32[]{:T(128)}, bf16[150,256,256]{2,1,0:T(8,128)(2,1)}, f32[18,16,150]{2,0,1:T(8,128)S(1)}, f32[18,256,150]{1,0,2:T(8,128)}, f32[256,18]{0,1:T(8,12...) while((s32[]{:T(128)}, ...), condition=%wide.region_13.14_spmd.clone, body=%wide.region_10.13_spmd.clone.sunk | while | flops 312124928 | bytes 24721096 | solution.py:195
  358.7 7.5 fusion.188
  368.0 10.4 fusion.190
  380.9 7.5 fusion.188
  390.2 10.4 fusion.190
  403.2 7.5 fusion.188
  412.4 10.4 fusion.190
  425.4 7.5 fusion.188
  434.7 10.4 fusion.190
  447.6 7.5 fusion.188
  456.9 10.4 fusion.190
  469.8 7.5 fusion.188
  479.1 10.4 fusion.190
  492.1 7.5 fusion.188
  501.3 10.4 fusion.190
  514.3 7.5 fusion.188
  523.6 10.4 fusion.190
  552.6 11.4 fusion.4
  567.9 6.9 fusion.60
  583.2 10.6 fusion.62
  593.9 12.5 multiply_reduce_fusion
  606.4 12.9 multiply_convert_fusion
  629.2 8.5 fusion.69
  637.7 68.6 %all-reduce.16.cloned.1.call-done = bf16[1176,1536]{0,1:T(8,128)(2,1)} async-done(((bf16[1176,1536]{0,1:T(8,128)(2,1)}), bf16[1176,1536]{0,1:T(8,128)(2,1)}) %all-reduce.16.cloned.1.call-update) | async-done | bytes 3612688
  708.3 6.2 fusion.73
  714.6 8.9 fusion.98
  723.6 7.0 fusion.141
  738.7 40.6 %reduce-scatter.13.cloned.1.call-done = f32[96,768]{1,0:T(8,128)} async-done(((f32[768,768]{1,0:T(8,128)}), f32[96,768]{1,0:T(8,128)}) %reduce-scatter.13.cloned.1.call-update) | async-done | bytes 294928 | tf_op jit(solution)/shard_map/reduce_scatter | solution.py:285
  781.0 130.1 %reduce-scatter.11.cloned.1.call-done = f32[96,2304]{1,0:T(8,128)} async-done(((f32[768,2304]{1,0:T(8,128)}), f32[96,2304]{1,0:T(8,128)}) %reduce-scatter.11.cloned.1.call-update) | async-done | bytes 884752 | tf_op jit(solution)/shard_map/reduce_scatter | solution.py:284
  913.1 164.4 %reduce-scatter.17.cloned.1.call-done = f32[384,768]{1,0:T(8,128)} async-done(((f32[3072,768]{1,0:T(8,128)}), f32[384,768]{1,0:T(8,128)}) %reduce-scatter.17.cloned.1.call-update) | async-done | bytes 1179664 | tf_op jit(solution)/shard_map/reduce_scatter | solution.py:289
  1079.6 164.2 %reduce-scatter.15.cloned.1.call-done = f32[96,3072]{1,0:T(8,128)} async-done(((f32[768,3072]{1,0:T(8,128)}), f32[96,3072]{1,0:T(8,128)}) %reduce-scatter.15.cloned.1.call-update) | async-done | bytes 1179664 | tf_op jit(solution)/shard_map/reduce_scatter | solution.py:288
  1246.6 39.5 %psum.63 = f32[150]{0:T(256)} all-reduce(f32[150]{0:T(256)S(1)} %get-tuple-element.312), channel_id=1, replica_groups=mesh['img'=8,'tile'=4] {'img','tile'}, use_global_device_ids=true, to_apply=%region_42.43 | all-reduce | flops 150 | bytes 1200 | tf_op jit(solution)/shard_map/psum | solution.py:208
  1286.1 21.8 %all-reduce.9 = (bf16[768]{0:T(1024)(128)(2,1)S(1)}, bf16[768]{0:T(1024)(128)(2,1)S(1)}) all-reduce(f32[768]{0:T(1024)S(1)} %get-tuple-element.310, f32[768]{0:T(1024)S(1)} %copy-done.27), channel_id=5, replica_groups=mesh['img'=8,'tile'=4] {'img'}, use_global_device_ids=true, to_apply=%region_28.29.clone | all-reduce | flops 1536 | bytes 9216
  1310.7 11.1 all-reduce.11
  1323.5 35.7 %all-reduce.18.cloned.1.call-done = (bf16[96,2304]{1,0:T(8,128)(2,1)}, bf16[96,768]{1,0:T(8,128)(2,1)}, bf16[96,3072]{1,0:T(8,128)(2,1)}, bf16[384,768]{1,0:T(8,128)(2,1)}) async-done(((bf16[96,2304]{1,0:T(8,128)(2,1)}, bf16[96,768]{1,0:T(8,128)(2,1)}, bf16[96,3072]{1,0:T(8,128)(2,1)}, bf16[384,768]{1,0:T(8,128)(2,1)}), (bf16[96,2304]{1,0:T(8,128)(2,1)}, bf16[96,768]{1,0:T(8,128)(2,1)}, ...) | async-done | bytes 1769488 | tf_op jit(solution)/shard_map/psum | solution.py:293
  (262 shorter events, 141.8 us)
Async XLA Ops:
  7.2 73.1 %all-gather.9.cloned.1.call-start = ((), (), s32[]{:S(2)}) async-start(), calls=%async_computation.5 | async-start | bytes 3981312 | tf_op jit(solution)/shard_map/all_gather | solution.py:110
  7.9 106.9 %all-gather.17.cloned.1.call-start = ((), (), s32[]{:S(2)}) async-start(), calls=%async_computation.13 | async-start | bytes 4546560 | tf_op jit(solution)/shard_map/all_gather | solution.py:64
  67.7 16.0 %copy-start.16 = (f32[768]{0:T(1024)}, f32[768]{0:T(1024)S(1)}, u32[]{:S(2)}) copy-start(f32[768]{0:T(1024)S(1)} %convert_element_type.194) | copy-start | bytes 9220
  67.8 90.3 %copy-start.6 = (bf16[38,768]{1,0:T(8,128)(2,1)}, bf16[38,768]{1,0:T(8,128)(2,1)S(1)}, u32[]{:S(2)}) copy-start(bf16[38,768]{1,0:T(8,128)(2,1)S(1)} %pad_dynamic-slice_fusion) | copy-start | bytes 175108
  69.0 14.8 %copy-start.19 = (f32[294]{0:T(512)}, f32[294]{0:T(512)S(1)}, u32[]{:S(2)}) copy-start(f32[294]{0:T(512)S(1)} %broadcast_multiply_fusion.1) | copy-start | bytes 3532
  70.3 13.5 copy-start.25
  70.3 13.5 copy-start.21
  83.8 3.6 copy-start.34
  84.8 73.3 %all-gather.11.cloned.1.call-start = ((), (), s32[]{:S(2)}) async-start(), calls=%async_computation.6 | async-start | bytes 1327104 | tf_op jit(solution)/shard_map/all_gather | solution.py:111
  85.6 153.3 %all-gather.13.cloned.1.call-start = ((), (), s32[]{:S(2)}) async-start(), calls=%async_computation.7 | async-start | bytes 5308416 | tf_op jit(solution)/shard_map/all_gather | solution.py:112
  86.1 232.8 %all-gather.15.cloned.1.call-start = ((), (), s32[]{:S(2)}) async-start(), calls=%async_computation.8 | async-start | bytes 5308416 | tf_op jit(solution)/shard_map/all_gather | solution.py:113
  86.7 619.6 %all-reduce.16.cloned.1.call-start = ((), (), s32[]{:S(2)}) async-start(), calls=%async_computation.15 | async-start | bytes 7864320
  87.5 53.0 %copy-start.30 = (pred[1176]{0:T(1024)(128)(4,1)}, pred[1176]{0:T(1024)(128)(4,1)S(1)}, u32[]{:S(2)}) copy-start(pred[1176]{0:T(1024)(128)(4,1)S(1)} %fusion.123) | copy-start | bytes 3532
  126.5 14.1 %copy-start.3 = (bf16[1176,768]{0,1:T(8,128)(2,1)}, bf16[1176,768]{0,1:T(8,128)(2,1)S(1)}, u32[]{:S(2)}) copy-start(bf16[1176,768]{0,1:T(8,128)(2,1)S(1)} %copy.48) | copy-start | bytes 5419012
  140.6 9.1 copy-start.23
  140.6 17.5 %copy-start.1 = (bf16[1,256,768]{2,1,0:T(8,128)(2,1)S(1)}, bf16[1,256,768]{2,1,0:T(8,128)(2,1)}, u32[]{:S(2)}) copy-start(bf16[1,256,768]{2,1,0:T(8,128)(2,1)} %param.17) | copy-start | bytes 1179652
  324.8 16.3 %copy-start.32 = (f32[38]{0:T(128)}, f32[38]{0:T(128)S(1)}, u32[]{:S(2)}) copy-start(f32[38]{0:T(128)S(1)} %multiply_reduce_fusion.8) | copy-start | bytes 460
  324.9 5.9 copy-start.28
  330.8 10.3 copy-start.8
  331.5 3.7 collective-permute-start
  333.7 3.9 collective-permute-start.1
  536.9 7.3 collective-permute-start.2
  542.9 3.1 collective-permute-start.3
  550.0 17.8 %copy-start.33 = (f32[38]{0:T(128)S(1)}, f32[38]{0:T(128)}, u32[]{:S(2)}) copy-start(f32[38]{0:T(128)} %copy-done.32) | copy-start | bytes 460
  550.0 17.9 %copy-start.29 = (f32[38]{0:T(128)S(1)}, f32[38]{0:T(128)}, u32[]{:S(2)}) copy-start(f32[38]{0:T(128)} %copy-done.28) | copy-start | bytes 460
  564.0 3.5 collective-permute-start.4
  567.9 12.9 copy-start.14
  574.9 5.5 copy-start.10
  574.9 5.9 copy-start.4
  580.8 2.5 copy-start.24
  583.2 10.6 copy-start.12
  619.3 3.7 copy-start
  619.3 3.7 copy-start.9
  625.2 154.1 %reduce-scatter.13.cloned.1.call-start = ((), (), s32[]{:S(2)}) async-start(), calls=%async_computation.10 | async-start | bytes 2654208 | tf_op jit(solution)/shard_map/reduce_scatter | solution.py:285
  628.5 282.6 %reduce-scatter.11.cloned.1.call-start = ((), (), s32[]{:S(2)}) async-start(), calls=%async_computation.9 | async-start | bytes 7962624 | tf_op jit(solution)/shard_map/reduce_scatter | solution.py:284
  629.2 79.1 %copy-start.2 = (bf16[1,256,768]{2,1,0:T(8,128)(2,1)S(1)}, bf16[1,256,768]{2,1,0:T(8,128)(2,1)}, u32[]{:S(2)}) copy-start(bf16[1,256,768]{2,1,0:T(8,128)(2,1)} %param.17) | copy-start | bytes 1179652
  629.2 79.1 %copy-start.7 = (bf16[38,768]{1,0:T(8,128)(2,1)S(1)}, bf16[38,768]{1,0:T(8,128)(2,1)}, u32[]{:S(2)}) copy-start(bf16[38,768]{1,0:T(8,128)(2,1)} %copy-done.6) | copy-start | bytes 175108
  629.2 79.1 %copy-start.17 = (f32[768]{0:T(1024)S(1)}, f32[768]{0:T(1024)}, u32[]{:S(2)}) copy-start(f32[768]{0:T(1024)} %copy-done.16) | copy-start | bytes 9220
  629.2 79.1 %copy-start.20 = (f32[294]{0:T(512)S(1)}, f32[294]{0:T(512)}, u32[]{:S(2)}) copy-start(f32[294]{0:T(512)} %copy-done.19) | copy-start | bytes 3532
  629.2 79.1 %copy-start.22 = (f32[294]{0:T(512)S(1)}, f32[294]{0:T(512)}, u32[]{:S(2)}) copy-start(f32[294]{0:T(512)} %copy-done.21) | copy-start | bytes 3532
  714.5 363.0 %reduce-scatter.17.cloned.1.call-start = ((), (), s32[]{:S(2)}) async-start(), calls=%async_computation.12 | async-start | bytes 10616832 | tf_op jit(solution)/shard_map/reduce_scatter | solution.py:289
  723.5 520.3 %reduce-scatter.15.cloned.1.call-start = ((), (), s32[]{:S(2)}) async-start(), calls=%async_computation.11 | async-start | bytes 10616832 | tf_op jit(solution)/shard_map/reduce_scatter | solution.py:288
  730.6 4.9 copy-start.26
  730.6 579.1 %reduce-scatter.19.cloned.1.call-start = ((), (), s32[]{:S(2)}) async-start(), calls=%async_computation.14 | async-start | bytes 884736
  738.6 547.5 %copy-start.27 = (f32[768]{0:T(1024)S(1)}, f32[768]{0:T(1024)}, u32[]{:S(2)}) copy-start(f32[768]{0:T(1024)} %get-tuple-element.308) | copy-start | bytes 9220
  738.6 620.5 %all-reduce.18.cloned.1.call-start = ((), (), s32[]{:S(2)}) async-start(), calls=%async_computation.16 | async-start | bytes 3538944 | tf_op jit(solution)/shard_map/psum | solution.py:293
  1359.1 4.4 copy-start.15
  1359.1 5.4 copy-start.18
  (4 other events, 5.9 us)
Sparse Core Ops, SparseCore 0:
  10.2 70.0 all-gather.8
  84.9 29.8 all-gather.16
  117.0 41.0 all-gather.10
  160.2 78.6 all-gather.12
  240.9 78.0 all-gather.14
  625.4 80.9 all-reduce.15
  709.8 69.4 reduce-scatter.12
  783.0 128.0 reduce-scatter.10
  915.1 162.3 reduce-scatter.16
  1081.4 162.3 reduce-scatter.14
  1248.0 61.5 reduce-scatter.18
  1313.3 45.8 all-reduce.17
where the time goes:
time: 1380 us; the launch traced here: 1370 us
  waiting for transfers between devices  807 us (58%)
  matrix products  276 us (20%)
  blocking collectives  145 us (11%)
  local copies, waits for them, and re-layouts  54.3 us (4%)
  other arithmetic  48.6 us (4%)
  between operations  18.5 us (1%)
    reduce_scatter x1, waiting for transfers between devices, shards(): lax.psum_scatter(w_back_grad, 'img', scatter_dimension=0, tiled=True)  164 us
    reduce_scatter x1, waiting for transfers between devices, shards(): lax.psum_scatter(w_in_grad, 'img', scatter_dimension=0, tiled=True)  164 us
    reduce_scatter x1, waiting for transfers between devices, shards(): lax.psum_scatter(w_qkv_grad, 'img', scatter_dimension=0, tiled=True)  130 us
    dot_general x8, matrix products, pixel_band(): jnp.einsum('cpq,qw->cpw', pixel_grad, across_table, precision=lax.Precisi...  82.9 us
    all_gather x1, waiting for transfers between devices, shards(): lax.all_gather(w_in, 'img', axis=0, tiled=True)  78.3 us
    all_gather x1, waiting for transfers between devices, shards(): lax.all_gather(w_back, 'img', axis=0, tiled=True)  74.3 us
    unnamed x15, waiting for transfers between devices  71.8 us
    dot_general x8, matrix products, pixel_band(): jnp.einsum('ph,hqc->cpq', row_band, cell_band, precision=lax.Precision.HI...  59.8 us
  transfers between devices with their start and end apart: 17, of which 14 were waited for; matrix products, arithmetic and copies ran while one was open for 8% of the time, Pallas kernels for 0%

commit v1 on v0

--- a/solution.py
+++ b/solution.py
@@ -1,11 +1,19 @@
+import functools
+
 import jax
 import jax.numpy as jnp
+import numpy as np
 from jax import lax
+from jax.experimental import pallas as pl
+from jax.experimental.pallas import tpu as pltpu
 from jax.sharding import PartitionSpec as P
 
 HEADS = 12
 WP = 16
 UP = 16
+BAND = 32
+BAND_CELLS = 4
+GROUP = 8
 
 
 def padded_2(x, sides, width):
@@ -48,11 +56,119 @@
     return value * lax.rsqrt(jnp.sum(value * value, axis=-1, keepdims=True) + 1e-06)
 
 
-def tent_table(pixel_first, pixels, cell_first, cells, total_cells):
-    place = ((pixel_first + jnp.arange(pixels)).astype(jnp.float32) + 0.5) / UP - 0.5
-    place = jnp.clip(place, 0.0, total_cells - 1.0)
-    grid_cells = (cell_first + jnp.arange(cells)).astype(jnp.float32)
-    return jnp.maximum(0.0, 1.0 - jnp.abs(place[:, None] - grid_cells[None, :]))
+def tent(pixels, cells, first):
+    place = (np.arange(pixels) + 0.5) / UP - 0.5 - first
+    return np.maximum(0.0, 1.0 - np.abs(place[:, None] - np.arange(cells)[None, :]))
+
+
+def band_tables():
+    across = (np.clip((np.arange(WP * UP) + 0.5) / UP - 0.5, 0, WP - 1))[None, :]
+    across = np.maximum(0.0, 1.0 - np.abs(across - np.arange(WP)[:, None]))
+    down = tent(BAND, BAND_CELLS, -1)
+    up = np.zeros((GROUP, BAND, 2, BAND_CELLS, GROUP), np.float32)
+    back = np.zeros((BAND_CELLS, GROUP, GROUP, BAND), np.float32)
+    for c in range(GROUP):
+        up[c, :, :, :, c] = down[:, None, :]
+        back[:, c, c, :] = down.T
+    up = up.reshape(GROUP * BAND, 2 * BAND_CELLS * GROUP)
+    back = back.reshape(BAND_CELLS * GROUP, GROUP * BAND)
+    return [jnp.asarray(t, jnp.bfloat16) for t in (across, up, back)]
+
+
+def two_parts(value):
+    high = value.astype(jnp.bfloat16)
+    return high, (value - high.astype(jnp.float32)).astype(jnp.bfloat16)
+
+
+def upsample_kernel(
+    classes, bands, cell_ref, label_ref, across_ref, up_ref, back_ref, mask_ref, sum_ref,
+    wide, wide_grad, powers,
+):
+    band = pl.program_id(0)
+    groups = -(-classes // GROUP)
+    tail = classes - GROUP * (groups - 1)
+    rows = cell_ref.shape[0] // WP
+    pixels = label_ref.shape[1]
+
+    @pl.when(band == 0)
+    def _():
+        for r in range(rows):
+            wide[r] = lax.dot_general(
+                cell_ref[WP * r : WP * (r + 1), :], across_ref[...], (((0,), (0,)), ((), ())),
+                preferred_element_type=jnp.float32,
+            )
+        wide_grad[...] = jnp.zeros_like(wide_grad)
+
+    step = BAND // UP
+
+    def forward(g, total, count):
+        part = wide[pl.ds(step * band, BAND_CELLS), pl.ds(GROUP * g, GROUP), :]
+        both = jnp.concatenate(two_parts(part.reshape(BAND_CELLS * GROUP, pixels)), axis=0)
+        upsampled = product(up_ref[: count * BAND, :], both).reshape(count, BAND, pixels)
+        mask_ref[pl.ds(GROUP * g, count)] = upsampled.astype(jnp.bfloat16)
+        power = jnp.exp(upsampled)
+        powers[pl.ds(GROUP * g, count)] = power
+        return total + jnp.sum(power, axis=0)
+
+    total = jnp.zeros((BAND, pixels), jnp.float32)
+    for g in range(groups):
+        total = forward(g, total, GROUP if g < groups - 1 else tail)
+    label = label_ref[...]
+    share = 1.0 / (UP * UP)
+    inverse = jnp.where(label >= 0, share, 0.0) / total
+
+    def backward(g, count):
+        parts = []
+        for c in range(count):
+            target = jnp.where(label == GROUP * g + c, share, 0.0)
+            parts.append((powers[GROUP * g + c] * inverse - target).astype(jnp.bfloat16))
+        summed = product(back_ref[:, : count * BAND], jnp.concatenate(parts, axis=0))
+        wide_grad[pl.ds(step * band, BAND_CELLS), pl.ds(GROUP * g, GROUP), :] += summed.reshape(
+            BAND_CELLS, GROUP, pixels
+        )
+
+    for g in range(groups):
+        backward(g, GROUP if g < groups - 1 else tail)
+
+    @pl.when(band == bands - 1)
+    def _():
+        for r in range(rows):
+            high, low = two_parts(wide_grad[r])
+            sum_ref[WP * r : WP * (r + 1), :] = times_transposed(
+                across_ref[...], high
+            ) + times_transposed(across_ref[...], low)
+
+
+def upsampled_loss(cells, label_grid, classes):
+    rows, lanes = cells.shape[0] // WP, cells.shape[1]
+    tile_pixels, wide_pixels = label_grid.shape
+    tables = band_tables()
+    bands = tile_pixels // BAND
+
+    def whole(shape):
+        return pl.BlockSpec(shape, lambda i: (0,) * len(shape))
+
+    return pl.pallas_call(
+        functools.partial(upsample_kernel, classes, bands),
+        grid=(bands,),
+        out_shape=(
+            jax.ShapeDtypeStruct((classes, tile_pixels, wide_pixels), jnp.bfloat16),
+            jax.ShapeDtypeStruct(cells.shape, jnp.float32),
+        ),
+        in_specs=[whole(cells.shape), pl.BlockSpec((BAND, wide_pixels), lambda i: (i, 0))]
+        + [whole(t.shape) for t in tables],
+        out_specs=(
+            pl.BlockSpec((classes, BAND, wide_pixels), lambda i: (0, i, 0)),
+            whole(cells.shape),
+        ),
+        scratch_shapes=[
+            pltpu.VMEM((rows, lanes, wide_pixels), jnp.float32),
+            pltpu.VMEM((rows, lanes, wide_pixels), jnp.float32),
+            pltpu.VMEM((lanes, BAND, wide_pixels), jnp.float32),
+        ],
+        compiler_params=pltpu.CompilerParams(vmem_limit_bytes=56 << 20),
+        name="upsampled_loss",
+    )(cells, label_grid, *tables)
 
 
 def forward_block(tokens, weights, key_valid):
@@ -146,60 +262,22 @@
     grid = normed.reshape(grid_rows, WP, classes)
     rimmed = padded_2(grid, (("tile", 0),), 1)
     tile_pixels = grid_rows * UP
-    wide_pixels = WP * UP
-    down_table = tent_table(
-        tile_index * tile_pixels,
-        tile_pixels,
-        tile_index * grid_rows - 1,
-        grid_rows + 2,
-        grid_rows * tile_count,
-    )
-    across_table = tent_table(0, wide_pixels, 0, WP, WP)
-    across_low = across_table.astype(jnp.bfloat16)
-    widened = jnp.einsum("hwc,qw->hqc", rimmed, across_low, preferred_element_type=jnp.float32)
-    band_rows = 32
-    band_cells = 4
     pixel_limit = height * UP - tile_index * tile_pixels
-    class_ids = jnp.arange(classes)[:, None, None]
-    label_grid = labels[0]
-
-    def pixel_band(block_index, carry):
-        mask_buffer, grid_sums = carry
-        first_row = block_index * band_rows
-        first_cell = first_row // UP
-        row_band = lax.dynamic_slice(down_table, (first_row, first_cell), (band_rows, band_cells))
-        cell_band = lax.dynamic_slice_in_dim(widened, first_cell, band_cells, 0)
-        upsampled = jnp.einsum("ph,hqc->cpq", row_band, cell_band, precision=lax.Precision.HIGHEST)
-        mask_buffer = lax.dynamic_update_slice_in_dim(
-            mask_buffer, upsampled.astype(jnp.bfloat16), first_row, 1
-        )
-        largest = jnp.max(upsampled, axis=0, keepdims=True)
-        powers = jnp.exp(upsampled - largest)
-        softmax_value = powers / jnp.sum(powers, axis=0, keepdims=True)
-        label_rows = lax.dynamic_slice_in_dim(label_grid, first_row, band_rows, 0)
-        target = (label_rows[None] == class_ids).astype(jnp.float32)
-        counted = (first_row + jnp.arange(band_rows) < pixel_limit).astype(jnp.float32)[
-            None, :, None
-        ]
-        pixel_grad = (softmax_value - target) * counted / (UP * UP)
-        narrowed = jnp.einsum(
-            "cpq,qw->cpw", pixel_grad, across_table, precision=lax.Precision.HIGHEST
-        )
-        cell_grad = jnp.einsum("ph,cpw->hwc", row_band, narrowed, precision=lax.Precision.HIGHEST)
-        current = lax.dynamic_slice_in_dim(grid_sums, first_cell, band_cells, 0)
-        grid_sums = lax.dynamic_update_slice_in_dim(grid_sums, current + cell_grad, first_cell, 0)
-        return (mask_buffer, grid_sums)
-
-    start_masks = jnp.zeros((classes, tile_pixels, wide_pixels), jnp.bfloat16)
-    start_sums = jnp.zeros((grid_rows + 2, WP, classes), jnp.float32)
-    mask_buffer, rim_grad = lax.fori_loop(
-        0, tile_pixels // band_rows, pixel_band, (start_masks, start_sums)
-    )
+    counted = jnp.arange(tile_pixels) < pixel_limit
+    label_grid = jnp.where(counted[:, None], labels[0], -1)
+    first = tile_index == 0
+    last = tile_index == tile_count - 1
+    rimmed = rimmed.at[0].set(jnp.where(first, rimmed[1], rimmed[0]))
+    rimmed = rimmed.at[-1].set(jnp.where(last, rimmed[-2], rimmed[-1]))
+    lanes = -(-classes // 16) * 16
+    cells = jnp.pad(rimmed.reshape(-1, classes), ((0, 0), (0, lanes - classes)))
+    mask_buffer, cell_sums = upsampled_loss(cells, label_grid, classes)
+    rim_grad = cell_sums[:, :classes].reshape(grid_rows + 2, WP, classes)
     rim_pair = jnp.stack([rim_grad[0], rim_grad[-1]], axis=0)
     incoming = padded_2(rim_pair, (("tile", 0),), 1)
     grid_grad = rim_grad[1:-1]
-    grid_grad = grid_grad.at[0].add(incoming[0])
-    grid_grad = grid_grad.at[-1].add(incoming[-1])
+    grid_grad = grid_grad.at[0].add(jnp.where(first, rim_grad[0], incoming[0]))
+    grid_grad = grid_grad.at[-1].add(jnp.where(last, rim_grad[-1], incoming[-1]))
     normed_grad = lax.optimization_barrier(
         grid_grad.reshape(own_rows, classes).astype(jnp.bfloat16)
     ).astype(jnp.float32)

time: 1380 us -> 1210 us (0.88)
  matrix products: 276 us -> 112 us
  local copies, waits for them, and re-layouts: 54.3 us -> 35.4 us
  Pallas kernels: 0 us -> 18.1 us
    dot_general x25 -> x0, matrix products: 162 us -> none  [the longest x8 82.9 us: pixel_band(): jnp.einsum('cpq,qw->cpw', pixel_grad, across_table, precision=lax.Precisi...]
    pallas_call x0 -> x1, Pallas kernels: none -> 18.1 us  [upsampled_loss(): pl.pallas_call(functools.partial(upsample_kernel, classes, bands), grid=(...]
  transfers between devices with their start and end apart: 17 -> 17, of which waited for: 14 -> 13; matrix products, arithmetic and copies ran while one was open for 8% -> 9% of each run, Pallas kernels for 0% -> 0%
where the time goes in v1:
time: 1210 us; the launch traced here: 1200 us
  waiting for transfers between devices  808 us (67%)
  blocking collectives  146 us (12%)
  matrix products  112 us (9%)
  other arithmetic  40 us (3%)
  local copies, waits for them, and re-layouts  35.4 us (3%)
  starting transfers between devices  22 us (2%)
  between operations  18.6 us (2%)
  Pallas kernels  18.1 us (1%)
    reduce_scatter x1, waiting for transfers between devices, shards(): lax.psum_scatter(w_back_grad, 'img', scatter_dimension=0, tiled=True)  164 us
    reduce_scatter x1, waiting for transfers between devices, shards(): lax.psum_scatter(w_in_grad, 'img', scatter_dimension=0, tiled=True)  164 us
    reduce_scatter x1, waiting for transfers between devices, shards(): lax.psum_scatter(w_qkv_grad, 'img', scatter_dimension=0, tiled=True)  130 us
    all_gather x1, waiting for transfers between devices, shards(): lax.all_gather(w_in, 'img', axis=0, tiled=True)  78.3 us
    all_gather x1, waiting for transfers between devices, shards(): lax.all_gather(w_back, 'img', axis=0, tiled=True)  74.3 us
    unnamed x15, waiting for transfers between devices  73.2 us
    unnamed x3, blocking collectives  55.7 us
    reduce_scatter x1, waiting for transfers between devices, shards(): lax.psum_scatter(w_out_grad, 'img', scatter_dimension=0, tiled=True)  40.4 us
  transfers between devices with their start and end apart: 17, of which 13 were waited for; matrix products, arithmetic and copies ran while one was open for 9% of the time, Pallas kernels for 0%

profile of v1, /device:TPU:0, one launch (start us, length us, event | category | flops | bytes accessed | tf_op | source)
XLA Modules:
  0.0 1200.1 jit_solution(13905557083757523497)
XLA Ops:
  8.0 33.8 %all-gather = bf16[8,96,150]{1,2,0:T(8,128)(2,1)S(1)} all-gather(bf16[1,96,150]{1,2,0:T(8,128)(2,1)} %bitcast.138), channel_id=1, replica_groups=mesh['img'=8,'tile'=4] {'img'}, dimensions={0}, use_global_device_ids=true | all-gather | bytes 259200 | tf_op jit(solution)/shard_map/all_gather | solution.py:232
  46.0 21.8 %all-reduce.11 = (bf16[768]{0:T(1024)(128)(2,1)S(1)}, bf16[768]{0:T(1024)(128)(2,1)S(1)}) all-reduce(bf16[768]{0:T(1024)(128)(2,1)S(1)} %dynamic-update-slice.12, bf16[768]{0:T(1024)(128)(2,1)S(1)} %dynamic-update-slice.13), channel_id=1, replica_groups=mesh['img'=8,'tile'=4] {'img'}, use_global_device_ids=true, to_apply=%add.3 | all-reduce | flops 1536 | bytes 6144
  70.3 9.9 all-gather.9.cloned.1.call-done
  80.3 3.4 convolution_convert_fusion
  87.8 27.0 %all-gather.17.cloned.1.call-done = bf16[4,294,1536]{2,1,0:T(8,128)(2,1)} async-done(((bf16[1,294,1536]{2,1,0:T(8,128)(2,1)}), bf16[4,294,1536]{2,1,0:T(8,128)(2,1)}) %all-gather.17.cloned.1.call-update) | async-done | bytes 3612688 | tf_op jit(solution)/shard_map/all_gather | solution.py:180
  114.8 4.8 reshape.359
  119.6 4.1 fusion.87
  123.7 2.7 copy.41
  126.4 4.2 copy.39
  130.6 10.0 exponential_reduce_fusion
  140.7 9.2 fusion.24
  149.9 8.2 all-gather.11.cloned.1.call-done
  160.5 78.3 %all-gather.13.cloned.1.call-done = bf16[768,3072]{1,0:T(8,128)(2,1)} async-done(((bf16[96,3072]{1,0:T(8,128)(2,1)}), bf16[768,3072]{1,0:T(8,128)(2,1)}) %all-gather.13.cloned.1.call-update) | async-done | bytes 4718608 | tf_op jit(solution)/shard_map/all_gather | solution.py:228
  238.8 5.8 fusion.84
  244.6 74.3 %all-gather.15.cloned.1.call-done = bf16[3072,768]{1,0:T(8,128)(2,1)} async-done(((bf16[384,768]{1,0:T(8,128)(2,1)}), bf16[3072,768]{1,0:T(8,128)(2,1)}) %all-gather.15.cloned.1.call-update) | async-done | bytes 4718608 | tf_op jit(solution)/shard_map/all_gather | solution.py:229
  318.9 5.7 convolution_add_fusion
  324.9 5.7 all-gather.2
  331.7 2.2 collective-permute-start
  333.9 12.9 %collective-permute-start.1 = (bf16[1,16,150]{2,1,0:T(8,128)(2,1)S(1)}, bf16[1,16,150]{2,1,0:T(8,128)(2,1)S(1)}, u32[]{:S(2)}, u32[]{:S(2)}) collective-permute-start(bf16[1,16,150]{2,1,0:T(8,128)(2,1)S(1)} %get-tuple-element.88), channel_id=1, source_target_pairs={{1,0},{2,1},{3,2},{5,4},{6,5},{7,6},{9,8},{10,9},{11,10},{13,12},{... | collective-permute-start | bytes 14408 | tf_op jit(solution)/shard_map/ppermute | solution.py:27
  348.4 18.1 %upsampled_loss.1 = (bf16[150,256,256]{2,1,0:T(8,128)(2,1)}, f32[288,160]{1,0:T(8,128)}) custom-call(bf16[288,160]{1,0:T(8,128)(2,1)} %pad.21.cell_ref, s32[256,256]{1,0:T(8,128)} %bitcast_select_fusion.label_ref, bf16[16,256]{1,0:T(8,128)(2,1)} %constant.215.clone.across_ref, bf16[256,64]{1,0:T(8,128)(2,1)} %constant.216.clone.up_ref, ...), custom_call_target="tpu_custom_call" | custom-call | tf_op jit(solution)/shard_map/upsampled_loss/pallas_call | solution.py:151
  367.3 3.8 collective-permute-start.2
  374.7 2.3 collective-permute-done.3
  379.8 12.2 %fusion = f32[40,768]{1,0:T(8,128)S(1)} fusion(f32[152,768]{1,0:T(8,128)} %pad.22), kind=kCustom, calls=%all-reduce-scatter | all-reduce-scatter fusion | flops 122881 | bytes 590336
  394.8 6.9 fusion.14
  401.7 4.9 multiply_reduce_fusion.1
  409.5 10.6 fusion.16
  420.2 12.5 %multiply_reduce_fusion = (f32[12,294]{1,0:T(8,128)S(1)}, f32[12,294,1176]{2,1,0:T(8,128)}) fusion(f32[12,294]{1,0:T(8,128)S(1)} %get-tuple-element.93, f32[12,294,1176]{2,1,0:T(8,128)} %get-tuple-element.94, bf16[294,12,64]{0,2,1:T(8,128)(2,1)S(1)} %bitcast.134, bf16[1176,12,64]{0,2,1:T(8,128)(2,1)} %bitcast.124), kind=kOutput, calls=%fused_computation.5 | convolution fusion | flops 543506048 | bytes 35477568 | tf_op jit(solution)/shard_map/qhd,khd->hqk/dot_general | solution.py:327
  432.6 13.0 %multiply_convert_fusion = bf16[12,294,1176]{2,1,0:T(8,128)(2,1)S(1)} fusion(f32[12,294,1176]{2,1,0:T(8,128)} %get-tuple-element.103, f32[12,294]{1,0:T(8,128)S(1)} %get-tuple-element.102, f32[12,294]{1,0:T(8,128)S(1)} %get-tuple-element.93, f32[12,294,1176]{2,1,0:T(8,128)} %get-tuple-element.94), kind=kLoop, calls=%fused_computation.4 | loop fusion | flops 16595712 | bytes 41517504 | tf_op jit(solution)/shard_map/convert_element_type | solution.py:333
  445.7 2.3 fusion.15
  449.4 2.2 pad_maximum_fusion
  452.6 2.2 fusion.40
  455.6 8.5 fusion.23
  464.1 69.9 %all-reduce.17.cloned.1.call-done = bf16[1176,1536]{0,1:T(8,128)(2,1)} async-done(((bf16[1176,1536]{0,1:T(8,128)(2,1)}), bf16[1176,1536]{0,1:T(8,128)(2,1)}) %all-reduce.17.cloned.1.call-update) | async-done | bytes 3612688
  535.9 6.2 fusion.27
  542.2 8.9 fusion.47
  551.2 7.0 fusion.83
  559.3 3.9 fusion.34
  566.3 40.4 %reduce-scatter.13.cloned.1.call-done = f32[96,768]{1,0:T(8,128)} async-done(((f32[768,768]{1,0:T(8,128)}), f32[96,768]{1,0:T(8,128)}) %reduce-scatter.13.cloned.1.call-update) | async-done | bytes 294928 | tf_op jit(solution)/shard_map/reduce_scatter | solution.py:363
  608.3 130.1 %reduce-scatter.11.cloned.1.call-done = f32[96,2304]{1,0:T(8,128)} async-done(((f32[768,2304]{1,0:T(8,128)}), f32[96,2304]{1,0:T(8,128)}) %reduce-scatter.11.cloned.1.call-update) | async-done | bytes 884752 | tf_op jit(solution)/shard_map/reduce_scatter | solution.py:362
  740.4 164.4 %reduce-scatter.17.cloned.1.call-done = f32[384,768]{1,0:T(8,128)} async-done(((f32[3072,768]{1,0:T(8,128)}), f32[384,768]{1,0:T(8,128)}) %reduce-scatter.17.cloned.1.call-update) | async-done | bytes 1179664 | tf_op jit(solution)/shard_map/reduce_scatter | solution.py:367
  907.0 164.3 %reduce-scatter.15.cloned.1.call-done = f32[96,3072]{1,0:T(8,128)} async-done(((f32[768,3072]{1,0:T(8,128)}), f32[96,3072]{1,0:T(8,128)}) %reduce-scatter.15.cloned.1.call-update) | async-done | bytes 1179664 | tf_op jit(solution)/shard_map/reduce_scatter | solution.py:366
  1071.3 2.2 convert_element_type.157
  1074.1 39.6 %psum.63 = f32[150]{0:T(256)} all-reduce(f32[150]{0:T(256)S(1)} %get-tuple-element.66), channel_id=1, replica_groups=mesh['img'=8,'tile'=4] {'img','tile'}, use_global_device_ids=true, to_apply=%region_38.39 | all-reduce | flops 150 | bytes 1200 | tf_op jit(solution)/shard_map/psum | solution.py:286
  1113.7 21.7 %all-reduce.10 = (bf16[768]{0:T(1024)(128)(2,1)S(1)}, bf16[768]{0:T(1024)(128)(2,1)S(1)}) all-reduce(f32[768]{0:T(1024)S(1)} %get-tuple-element.64, f32[768]{0:T(1024)S(1)} %get-tuple-element.62), channel_id=5, replica_groups=mesh['img'=8,'tile'=4] {'img'}, use_global_device_ids=true, to_apply=%region_24.25.clone | all-reduce | flops 1536 | bytes 9216
  1138.3 11.1 all-reduce.12
  1151.1 35.7 %all-reduce.19.cloned.1.call-done = (bf16[96,2304]{1,0:T(8,128)(2,1)}, bf16[96,768]{1,0:T(8,128)(2,1)}, bf16[96,3072]{1,0:T(8,128)(2,1)}, bf16[384,768]{1,0:T(8,128)(2,1)}) async-done(((bf16[96,2304]{1,0:T(8,128)(2,1)}, bf16[96,768]{1,0:T(8,128)(2,1)}, bf16[96,3072]{1,0:T(8,128)(2,1)}, bf16[384,768]{1,0:T(8,128)(2,1)}), (bf16[96,2304]{1,0:T(8,128)(2,1)}, bf16[96,768]{1,0:T(8,128)(2,1)}, ...) | async-done | bytes 1769488 | tf_op jit(solution)/shard_map/psum | solution.py:371
  1186.7 2.2 convert_element_type.158
  1189.0 2.2 convert_element_type.160
  (158 shorter events, 48.1 us)
Async XLA Ops:
  7.2 73.1 %all-gather.9.cloned.1.call-start = ((), (), s32[]{:S(2)}) async-start(), calls=%async_computation.5 | async-start | bytes 3981312 | tf_op jit(solution)/shard_map/all_gather | solution.py:226
  7.9 106.9 %all-gather.17.cloned.1.call-start = ((), (), s32[]{:S(2)}) async-start(), calls=%async_computation.13 | async-start | bytes 4546560 | tf_op jit(solution)/shard_map/all_gather | solution.py:180
  70.3 13.4 %copy-start.16 = (f32[294]{0:T(512)}, f32[294]{0:T(512)S(1)}, u32[]{:S(2)}) copy-start(f32[294]{0:T(512)S(1)} %fusion.33) | copy-start | bytes 3532
  83.7 3.6 copy-start.18
  84.8 73.3 %all-gather.11.cloned.1.call-start = ((), (), s32[]{:S(2)}) async-start(), calls=%async_computation.6 | async-start | bytes 1327104 | tf_op jit(solution)/shard_map/all_gather | solution.py:227
  85.5 153.3 %all-gather.13.cloned.1.call-start = ((), (), s32[]{:S(2)}) async-start(), calls=%async_computation.7 | async-start | bytes 5308416 | tf_op jit(solution)/shard_map/all_gather | solution.py:228
  86.1 232.8 %all-gather.15.cloned.1.call-start = ((), (), s32[]{:S(2)}) async-start(), calls=%async_computation.8 | async-start | bytes 5308416 | tf_op jit(solution)/shard_map/all_gather | solution.py:229
  86.7 447.3 %all-reduce.17.cloned.1.call-start = ((), (), s32[]{:S(2)}) async-start(), calls=%async_computation.15 | async-start | bytes 7864320
  87.8 52.8 %copy-start.3 = (bf16[294,768]{0,1:T(8,128)(2,1)}, bf16[294,768]{0,1:T(8,128)(2,1)S(1)}, u32[]{:S(2)}) copy-start(bf16[294,768]{0,1:T(8,128)(2,1)S(1)} %copy.40) | copy-start | bytes 1354756
  126.4 14.2 %copy-start.2 = (bf16[1176,768]{0,1:T(8,128)(2,1)}, bf16[1176,768]{0,1:T(8,128)(2,1)S(1)}, u32[]{:S(2)}) copy-start(bf16[1176,768]{0,1:T(8,128)(2,1)S(1)} %copy.41) | copy-start | bytes 5419012
  140.6 17.4 %copy-start.1 = (bf16[1,256,768]{2,1,0:T(8,128)(2,1)S(1)}, bf16[1,256,768]{2,1,0:T(8,128)(2,1)}, u32[]{:S(2)}) copy-start(bf16[1,256,768]{2,1,0:T(8,128)(2,1)} %param.22) | copy-start | bytes 1179652
  324.6 22.2 %copy-start.14 = (s32[1,256,256]{2,1,0:T(8,128)S(1)}, s32[1,256,256]{2,1,0:T(8,128)}, u32[]{:S(2)}) copy-start(s32[1,256,256]{2,1,0:T(8,128)} %param.23) | copy-start | bytes 786436
  331.7 16.0 %collective-permute-start = (bf16[1,16,150]{2,1,0:T(8,128)(2,1)S(1)}, bf16[1,16,150]{2,1,0:T(8,128)(2,1)S(1)}, u32[]{:S(2)}, u32[]{:S(2)}) collective-permute-start(bf16[1,16,150]{2,1,0:T(8,128)(2,1)S(1)} %get-tuple-element.87), channel_id=1, source_target_pairs={{0,1},{1,2},{2,3},{4,5},{5,6},{6,7},{8,9},{9,10},{10,11},{12,13},{... | collective-permute-start | bytes 14408 | tf_op jit(solution)/shard_map/ppermute | solution.py:26
  333.9 13.7 %collective-permute-start.1 = (bf16[1,16,150]{2,1,0:T(8,128)(2,1)S(1)}, bf16[1,16,150]{2,1,0:T(8,128)(2,1)S(1)}, u32[]{:S(2)}, u32[]{:S(2)}) collective-permute-start(bf16[1,16,150]{2,1,0:T(8,128)(2,1)S(1)} %get-tuple-element.88), channel_id=1, source_target_pairs={{1,0},{2,1},{3,2},{5,4},{6,5},{7,6},{9,8},{10,9},{11,10},{13,12},{... | collective-permute-start | bytes 14408 | tf_op jit(solution)/shard_map/ppermute | solution.py:27
  367.3 6.7 collective-permute-start.2
  372.7 4.3 collective-permute-start.3
  392.0 2.4 collective-permute-start.4
  394.8 12.3 %copy-start.12 = (f32[38,768]{1,0:T(8,128)}, f32[38,768]{1,0:T(8,128)S(1)}, u32[]{:S(2)}) copy-start(f32[38,768]{1,0:T(8,128)S(1)} %add_add_fusion.6) | copy-start | bytes 350212
  401.7 4.9 copy-start.8
  401.7 5.4 copy-start.5
  406.6 1.3 copy-start.9
  407.1 2.5 copy-start.4
  409.5 10.6 copy-start.10
  445.6 3.7 copy-start
  445.6 3.7 copy-start.7
  451.6 1.1 copy-start.11
  451.6 155.1 %reduce-scatter.13.cloned.1.call-start = ((), (), s32[]{:S(2)}) async-start(), calls=%async_computation.10 | async-start | bytes 2654208 | tf_op jit(solution)/shard_map/reduce_scatter | solution.py:363
  454.8 283.6 %reduce-scatter.11.cloned.1.call-start = ((), (), s32[]{:S(2)}) async-start(), calls=%async_computation.9 | async-start | bytes 7962624 | tf_op jit(solution)/shard_map/reduce_scatter | solution.py:362
  542.1 362.7 %reduce-scatter.17.cloned.1.call-start = ((), (), s32[]{:S(2)}) async-start(), calls=%async_computation.12 | async-start | bytes 10616832 | tf_op jit(solution)/shard_map/reduce_scatter | solution.py:367
  551.1 520.2 %reduce-scatter.15.cloned.1.call-start = ((), (), s32[]{:S(2)}) async-start(), calls=%async_computation.11 | async-start | bytes 10616832 | tf_op jit(solution)/shard_map/reduce_scatter | solution.py:366
  558.2 1.1 copy-start.6
  558.2 4.9 copy-start.17
  558.2 579.0 %reduce-scatter.19.cloned.1.call-start = ((), (), s32[]{:S(2)}) async-start(), calls=%async_computation.14 | async-start | bytes 884736
  566.3 620.4 %all-reduce.19.cloned.1.call-start = ((), (), s32[]{:S(2)}) async-start(), calls=%async_computation.16 | async-start | bytes 3538944 | tf_op jit(solution)/shard_map/psum | solution.py:371
  1186.7 4.4 copy-start.13
  1186.7 5.4 copy-start.15
Sparse Core Ops, SparseCore 0:
  10.2 70.0 all-gather.8
  84.9 29.8 all-gather.16
  117.0 41.0 all-gather.10
  160.1 78.6 all-gather.12
  240.8 78.0 all-gather.14
  451.7 82.2 all-reduce.16
  537.5 69.1 reduce-scatter.12
  610.4 128.0 reduce-scatter.10
  742.4 162.3 reduce-scatter.16
  908.7 162.5 reduce-scatter.14
  1075.5 61.6 reduce-scatter.18
  1140.9 45.8 all-reduce.18

commit v2 on v1

v2 whole, which is shorter than its diff:
```python
import collections
import functools
import types

import jax
import jax.numpy as jnp
import numpy as np
from jax import lax
from jax.experimental import pallas as pl
from jax.experimental.pallas import tpu as pltpu
from jax.sharding import PartitionSpec as P

IMG = "img"
TILE = "tile"
HEADS = 12
WP = 16
UP = 16
BAND = 32
BAND_CELLS = 4
GROUP = 8
MESH = pl.DeviceIdType.MESH
F32 = jnp.float32
BF16 = jnp.bfloat16
PLANE = 2
BACK, INTO, JOINT = 0, 1, 2
VMEM_BYTES = 62 << 20


def product(left, right):
    return jnp.dot(left, right, preferred_element_type=F32)


def times_transposed(left, right):
    return lax.dot_general(left, right, (((1,), (1,)), ((), ())), preferred_element_type=F32)


def transposed_times(left, right):
    return lax.dot_general(left, right, (((0,), (0,)), ((), ())), preferred_element_type=F32)


def layer_norm_parts(value):
    centre = jnp.mean(value, axis=-1, keepdims=True)
    centred = value - centre
    spread = jnp.mean(centred * centred, axis=-1, keepdims=True)
    scale = lax.rsqrt(spread + 1e-05)
    return centred * scale, scale


def layer_norm_back(unit, scale, gain, upstream):
    weighted = upstream * gain
    mean = jnp.mean(weighted, axis=-1, keepdims=True)
    along = jnp.mean(weighted * unit, axis=-1, keepdims=True)
    gain_row = jnp.sum(upstream * unit, axis=0, keepdims=True)
    return scale * (weighted - mean - unit * along), gain_row


def gelu_pair(x):
    root = np.float32(np.sqrt(2.0 / np.pi))
    square = x * x
    turned = jnp.tanh(root * x * (1.0 + np.float32(0.044715) * square))
    half = 0.5 * (1.0 + turned)
    slope = half + 0.5 * x * (1.0 - turned * turned) * root * (
        1.0 + np.float32(3 * 0.044715) * square
    )
    return x * half, slope


def lane_iota(rows, lanes):
    return lax.broadcasted_iota(jnp.int32, (rows, lanes), 1)


def row_iota(rows, lanes):
    return lax.broadcasted_iota(jnp.int32, (rows, lanes), 0)


class Net:
    def __init__(self, k):
        self.k = k
        self.sent = []
        self.stage_sends = []

    def send(self, source, target, base, slot, device, when=None):
        k = self.k
        copy = pltpu.make_async_remote_copy(
            src_ref=source,
            dst_ref=target,
            send_sem=k.send_sem.at[len(self.sent)],
            recv_sem=k.recv_sem.at[base + slot],
            device_id=device,
            device_id_type=MESH,
        )
        self.sent.append((copy, when))
        if when is None:
            copy.start()
        else:
            pl.when(when)(copy.start)
        return len(self.sent) - 1

    def arrived(self, target, base, slot):
        k = self.k
        pltpu.make_async_remote_copy(
            src_ref=target,
            dst_ref=target,
            send_sem=k.send_sem.at[0],
            recv_sem=k.recv_sem.at[base + slot],
            device_id=k.sibling,
            device_id_type=MESH,
        ).wait_recv()

    def gone(self, number):
        if self.sent[number] is None:
            return
        copy, when = self.sent[number]
        self.sent[number] = None
        if when is None:
            copy.wait_send()
        else:
            pl.when(when)(copy.wait_send)

    def drain(self):
        for number in range(len(self.sent)):
            self.gone(number)


def place(k):
    k.i = lax.axis_index(IMG)
    k.t = lax.axis_index(TILE)
    k.y = k.i % PLANE
    k.z = k.i // PLANE
    k.planes = k.s.images // PLANE
    k.ts = k.t + 1 - 2 * (k.t % 2)
    k.tx = (k.t + 2) % 4
    k.td = (k.ts + 2) % 4
    k.sibling = (k.i, k.ts)
    k.across = (k.i, k.tx)
    k.diagonal = (k.i, k.td)
    k.mate = (k.i + 1 - 2 * k.y, k.t)


def line_peer(k, step):
    z = (k.z + step) % k.planes
    return z, (PLANE * z + k.y, k.t)


def enter(k):
    barrier = pltpu.get_barrier_semaphore()
    peers = [k.sibling, k.across, k.diagonal]
    if k.s.img_comm:
        peers += [k.mate] + [line_peer(k, step)[1] for step in range(1, k.planes)]
    for peer in peers:
        pl.semaphore_signal(barrier, inc=1, device_id=peer, device_id_type=MESH)
    pl.semaphore_wait(barrier, len(peers))


def spread_start(k, own, slots, name):
    for step in range(1, k.planes):
        k.net.send(own, slots.at[k.i], name, k.i, line_peer(k, step)[1])
    k.net.send(own, slots.at[k.i], name, k.i, k.mate)


def spread_pass(k, slots, name):
    for step in range(1, k.planes):
        z = (k.z + k.planes - step) % k.planes
        i = PLANE * z + k.y
        k.net.arrived(slots.at[i], name, i)
        k.net.send(slots.at[i], slots.at[i], name, i, k.mate)


def spread_end(k, slots, name):
    for z in range(k.planes):
        i = PLANE * z + 1 - k.y
        k.net.arrived(slots.at[i], name, i)


def slot_part(slots, slot, rows):
    return slots.at[slot] if rows is None else slots.at[slot, rows]


def share_start(k, slots, base, rows=None):
    own = slot_part(slots, k.t, rows)
    k.net.send(own, own, base, k.t, k.across)
    k.net.send(own, own, base, k.t, k.sibling)


def share_pass(k, slots, base, rows=None):
    part = slot_part(slots, k.tx, rows)
    k.net.arrived(part, base, k.tx)
    k.net.send(part, part, base, k.tx, k.sibling)


def reduce_over_tile(k, name, part, before):
    sends = k.net.stage_sends
    for number in sends:
        k.net.gone(number)
    sends.clear()
    k.own_part[...] = part(k.t)
    before(k.ts)
    k.stage[0] = part(k.ts).astype(BF16)
    sends.append(k.net.send(k.stage.at[0], k.from_sib.at[0], name, 0, k.sibling))
    before(k.tx)
    k.across_part[...] = part(k.tx)
    before(k.td)
    k.stage[1] = part(k.td).astype(BF16)
    sends.append(k.net.send(k.stage.at[1], k.from_sib.at[1], name, 1, k.sibling))
    k.net.arrived(k.from_sib.at[1], name, 1)
    k.stage[2] = (k.across_part[...] + k.from_sib[1].astype(F32)).astype(BF16)
    sends.append(k.net.send(k.stage.at[2], k.from_across, name, 2, k.across))


def reduced_over_tile(k, name):
    k.net.arrived(k.from_sib.at[0], name, 0)
    k.net.arrived(k.from_across, name, 2)
    return k.own_part[...] + k.from_sib[0].astype(F32) + k.from_across[...].astype(F32)


def key_bias(k, slot, height):
    s = k.s
    rows = row_iota(s.rows, s.head)
    cls = rows - s.own
    patch_ok = (rows < s.own) & (rows < (height - slot * s.grid) * WP)
    class_ok = (cls >= 0) & (cls < s.step) & (slot * s.step + cls < s.classes)
    off = jnp.where(patch_ok | class_ok, 0.0, -1e30)
    return jnp.where(lane_iota(s.rows, s.head) == 0, off, 0.0)


def class_rows(k, slot):
    s = k.s
    rows = k.cls_rows[pl.ds(pl.multiple_of(slot * s.step, 8), s.step), :]
    return jnp.concatenate([rows, jnp.zeros((s.slot - s.step, s.dim), F32)], axis=0)


def slot_rows(k, slot):
    return pl.ds(pl.multiple_of(slot * k.s.rows, 16), k.s.rows)


def block_scores(k, head, slot):
    return times_transposed(k.q[head, slot_rows(k, slot), :], k.keys[head])


def deal_start(k, own, slots, base):
    mine = k.z == k.t

    @pl.when(mine)
    def _():
        slots[k.t, k.y] = own[...]

    for step in range(1, k.planes):
        k.net.send(own, slots.at[k.t, k.y], base, 0, line_peer(k, step)[1], mine)


def deal_pass(k, slots, base):
    @pl.when(k.z != k.t)
    def _():
        k.net.arrived(slots.at[k.t, k.y], base, 0)

    k.net.send(slots.at[k.t, k.y], slots.at[k.t, k.y], base, 1, k.mate)


def deal_end(k, slots, base):
    k.net.arrived(slots.at[k.t, 1 - k.y], base, 1)


def pick_columns(k):
    s = k.s
    wide, part = s.here * s.head, s.hidden // s.images
    for n in range(4):

        @pl.when(k.t == n)
        def _(n=n):
            cut = [
                k.w_qkv[:, s.dim * m + wide * n + s.head * h :][:, : s.head]
                for h in range(s.here)
                for m in range(3)
            ]
            k.wq[...] = jnp.concatenate(cut, axis=1)
            cut = [k.w_in[:, part * (4 * i + n) :][:, :part] for i in range(s.images)]
            k.wi[...] = jnp.concatenate(cut, axis=1)


def forward_kernel(k):
    s = k.s
    place(k)
    net = k.net
    i, t = k.i, k.t
    head_gain = k.gain_row[...].astype(F32)
    head_gain = jnp.concatenate([head_gain, jnp.zeros((1, s.lanes - s.classes), F32)], axis=1)
    k.head_gain[...] = jnp.broadcast_to(head_gain, (8, s.lanes))
    if s.img_comm:
        shard = s.dim // s.images
        rows = [ref[...].astype(F32) for ref in (k.cls_emb, k.gain_one, k.gain_two)]
        rows += [jnp.zeros((s.lanes - s.classes - 2, shard), F32)]
        table = jnp.concatenate(rows, axis=0)
        table = jnp.concatenate([table, jnp.zeros((s.lanes, 128 - shard), F32)], axis=1)
        k.small[...] = table.astype(BF16)
        k.smalls[i] = table.astype(BF16)
        pick_columns(k)
    enter(k)
    if s.img_comm:
        spread_start(k, k.small, k.smalls, k.at.small)
    k.tokens[t] = k.patches[0]
    net.send(k.patches.at[0], k.tokens.at[t], k.at.tokens, t, k.across)
    net.send(k.patches.at[0], k.tokens.at[t], k.at.tokens, t, k.sibling)
    if s.img_comm:
        spread_start(k, k.wq, k.w_joint, k.at.w_joint)
        k.w_joint[i] = k.wq[...]
        k.w_expand[i] = k.wi[...]
        k.w_reduce[i] = k.wb[t]
        spread_pass(k, k.smalls, k.at.small)
        spread_end(k, k.smalls, k.at.small)
        pieces = [k.smalls[n].astype(F32)[:, :shard] for n in range(s.images)]
        full = jnp.concatenate(pieces, axis=1)
    else:
        full = k.small_full[...].astype(F32)
    k.gains[0:2] = full[s.classes : s.classes + 2]
    k.cls_rows[...] = jnp.where(row_iota(s.lanes, s.dim) < s.classes, full, 0.0)
    gain_one, gain_two = k.gains[0:1], k.gains[1:2]

    def normed_tokens(slot):
        value = jnp.concatenate([k.tokens[slot].astype(F32), class_rows(k, slot)], axis=0)
        k.h_one[slot] = (layer_norm_parts(value)[0] * gain_one).astype(BF16)

    k.token_rows[0 : s.own] = k.patches[0].astype(F32)
    k.token_rows[s.own : s.rows] = class_rows(k, t)
    normed_tokens(t)
    net.arrived(k.tokens.at[k.ts], k.at.tokens, k.ts)
    normed_tokens(k.ts)
    net.arrived(k.tokens.at[k.tx], k.at.tokens, k.tx)
    net.send(k.tokens.at[k.tx], k.tokens.at[k.tx], k.at.tokens, k.tx, k.sibling)
    normed_tokens(k.tx)
    if s.img_comm:
        spread_pass(k, k.w_joint, k.at.w_joint)
        deal_start(k, k.wo, k.w_project, k.at.w_project)
        spread_start(k, k.wi, k.w_expand, k.at.w_expand)
    net.arrived(k.tokens.at[k.td], k.at.tokens, k.td)
    normed_tokens(k.td)
    if s.img_comm:
        spread_end(k, k.w_joint, k.at.w_joint)

    lane = lane_iota(s.rows, s.head)
    one = jnp.where(lane == 0, 1.0, 0.0)
    ones = jnp.where(lane < 2, 1.0, 0.0)
    height = k.height[0]

    def joint(slot, carry):
        value = product(k.h_one[slot], k.w_joint[...].reshape(s.dim, s.here * 3 * s.head))
        bias = key_bias(k, slot, height)
        rows = slot_rows(k, slot)
        for h in range(s.here):
            cut = [
                value[:, (3 * h + n) * s.head : (3 * h + n + 1) * s.head] for n in range(3)
            ]
            for ref, part, extra in zip(
                (k.q, k.keys, k.values), (cut[0] * s.head**-0.5, cut[1], cut[2]), (one, bias, ones)
            ):
                ref[h, rows, :] = jnp.concatenate([part, extra], axis=1).astype(BF16)
        return carry

    lax.fori_loop(0, 4, joint, 0)

    def attend(slot):
        rows = slot_rows(k, slot)
        wide_lane = lane_iota(s.rows, 2 * s.head)
        parts = []
        for h in range(s.here):
            scores = block_scores(k, h, slot)
            largest = jnp.max(scores, axis=-1, keepdims=True)
            powers = jnp.exp(scores - largest).astype(BF16)
            out = product(powers, k.values[h])
            parts.append(out[:, : s.head] / out[:, s.head : s.head + 1])
            k.outs[h, rows, :] = jnp.where(wide_lane == s.head + 1, largest, out)
        k.mixed[slot] = jnp.concatenate(parts, axis=1).astype(BF16)

    for step in range(1, 5):
        slot = (t + step) % 4
        attend(slot)
        if step < 4:
            net.send(k.mixed.at[slot], k.mixed_all.at[t], k.at.mixed, t, (i, slot))
        if s.img_comm:
            if step == 2:
                deal_pass(k, k.w_project, k.at.w_project)
            if step == 3:
                spread_start(k, k.wb.at[t], k.w_reduce, k.at.w_reduce)
    k.mixed_all[t] = k.mixed[t]
    if s.img_comm:
        deal_end(k, k.w_project, k.at.w_project)
        share_start(k, k.w_project, k.at.w_shared)
        spread_pass(k, k.w_expand, k.at.w_expand)
        share_pass(k, k.w_project, k.at.w_shared)
        net.arrived(k.w_project.at[k.ts], k.at.w_shared, k.ts)
        net.arrived(k.w_project.at[k.td], k.at.w_shared, k.td)
    after = k.token_rows[...]
    w_project = k.w_project[...].reshape(s.dim, s.dim)
    for step in range(1, 4):
        slot = (t + step) % 4
        net.arrived(k.mixed_all.at[slot], k.at.mixed, slot)
    wide = s.here * s.head
    for n in range(4):
        after = after + product(k.mixed_all[n], w_project[wide * n : wide * (n + 1)])
    k.after[...] = after
    k.h_two[t] = (layer_norm_parts(after)[0] * gain_two).astype(BF16)
    share_start(k, k.h_two, k.at.h_two)
    if s.img_comm:
        spread_end(k, k.w_expand, k.at.w_expand)
        spread_pass(k, k.w_reduce, k.at.w_reduce)
        spread_end(k, k.w_reduce, k.at.w_reduce)

    def feed(slot):
        pre = product(k.h_two[slot], k.w_expand[...].reshape(s.dim, s.hidden))
        act, slope = gelu_pair(pre)
        act = act.astype(BF16)
        k.act[slot] = act
        k.slope[slot] = slope.astype(BF16)
        return product(act, k.w_reduce[...].reshape(s.hidden, s.dim))

    def ready(slot):
        if slot is k.tx:
            share_pass(k, k.h_two, k.at.h_two)
        else:
            net.arrived(k.h_two.at[slot], k.at.h_two, slot)

    reduce_over_tile(k, k.at.feed, feed, ready)
    final = k.after[...] + reduced_over_tile(k, k.at.feed)
    k.final[...] = final
    unit = (final * lax.rsqrt(jnp.sum(final * final, axis=-1, keepdims=True) + 1e-06)).astype(BF16)
    k.cls_units[t] = unit[s.own :]
    k.patch_unit[WP : WP + s.own] = unit[: s.own]
    top, bottom = pl.ds(0, WP), pl.ds(WP + s.own, WP)
    for slot in (k.tx, k.td, k.ts):
        net.send(k.cls_units.at[t], k.cls_units.at[t], k.at.units, t, (i, slot))
    net.send(k.patch_unit.at[pl.ds(WP, WP)], k.patch_unit.at[bottom], k.at.rim, 1, (i, (t + 3) % 4))
    net.send(k.patch_unit.at[pl.ds(s.own, WP)], k.patch_unit.at[top], k.at.rim, 0, (i, (t + 1) % 4))
    for slot in (k.ts, k.tx, k.td):
        net.arrived(k.cls_units.at[slot], k.at.units, slot)
    net.arrived(k.patch_unit.at[top], k.at.rim, 0)
    net.arrived(k.patch_unit.at[bottom], k.at.rim, 1)
    units = jnp.concatenate([k.cls_units[n].astype(F32)[: s.step] for n in range(4)], axis=0)
    units = jnp.where(row_iota(s.lanes, s.dim) < s.classes, units, 0.0).astype(BF16)
    k.class_unit[...] = units
    logits = times_transposed(k.patch_unit[...], units)
    unit_logits, scale = class_norm_parts(k, logits)
    k.logit_unit[...] = unit_logits[WP : WP + s.own]
    k.logit_scale[...] = jnp.broadcast_to(scale[WP : WP + s.own], (s.own, 128))
    normed = (unit_logits * k.head_gain[0:1]).astype(BF16)
    k.cells[WP : WP + s.own] = normed[WP : WP + s.own]
    k.cells[:WP] = jnp.where(t == 0, normed[WP : 2 * WP], normed[:WP])
    k.cells[WP + s.own :] = jnp.where(t == 3, normed[s.own : WP + s.own], normed[WP + s.own :])
    net.drain()


def class_norm_parts(k, value):
    s = k.s
    real = lane_iota(value.shape[0], s.lanes) < s.classes
    centre = jnp.sum(value, axis=-1, keepdims=True) / s.classes
    centred = jnp.where(real, value - centre, 0.0)
    spread = jnp.sum(centred * centred, axis=-1, keepdims=True) / s.classes
    scale = lax.rsqrt(spread + 1e-05)
    return centred * scale, scale


def sum_start(k, name):
    g = k.grads[name]
    k.net.send(g.blocks.at[1 - k.y], g.from_mate, g.at_mate, 0, k.mate)


def sum_pass(k, name):
    g = k.grads[name]
    k.net.arrived(g.from_mate, g.at_mate, 0)
    for step in range(k.planes):
        z = (k.z + step) % k.planes
        both = g.blocks[k.y, z].astype(F32) + g.from_mate[z].astype(F32)
        g.both[z] = both.astype(BF16)
        if step:
            k.net.send(g.both.at[z], g.from_line.at[k.z], g.at_line, k.z, line_peer(k, step)[1])


def sum_end(k, name):
    g = k.grads[name]
    total = g.both[k.z].astype(F32)
    for step in range(1, k.planes):
        z = (k.z + step) % k.planes
        k.net.arrived(g.from_line.at[z], g.at_line, z)
        total = total + g.from_line[z].astype(F32)
    g.out[k.t] = total.astype(BF16)
    share_start(k, g.out, g.at_out)


def sum_share(k, name):
    g = k.grads[name]
    share_pass(k, g.out, g.at_out)


def sum_close(k, name):
    g = k.grads[name]
    k.net.arrived(g.out.at[k.ts], g.at_out, k.ts)
    k.net.arrived(g.out.at[k.td], g.at_out, k.td)


def put_blocks(k, name, value):
    g = k.grads[name]
    if not k.s.img_comm:
        g.out[...] = value.astype(BF16)
        return
    rows = value.shape[0] // k.s.images
    for i in range(k.s.images):
        g.blocks[i % PLANE, i // PLANE] = value[rows * i : rows * (i + 1)].astype(BF16)


def backward_kernel(k):
    s = k.s
    place(k)
    enter(k)
    net = k.net
    i, t = k.i, k.t
    comm = s.img_comm
    patch_part, class_part = pl.ds(0, s.own), pl.ds(s.own, s.slot)

    net.send(k.cell_sums.at[0:WP], k.rim_in.at[1], k.at.rim, 1, (i, (t + 3) % 4))
    net.send(k.cell_sums.at[WP + s.own : 2 * WP + s.own], k.rim_in.at[0], k.at.rim, 0, (i, (t + 1) % 4))
    net.arrived(k.rim_in.at[0], k.at.rim, 0)
    net.arrived(k.rim_in.at[1], k.at.rim, 1)
    top = jnp.where(t == 0, k.cell_sums[:WP], k.rim_in[0])
    bottom = jnp.where(t == 3, k.cell_sums[WP + s.own :], k.rim_in[1])
    own = k.cell_sums[WP : WP + s.own]
    own = jnp.concatenate(
        [own[:WP] + top, own[WP : s.own - WP], own[s.own - WP :] + bottom], axis=0
    )
    upstream = own.astype(BF16).astype(F32)
    unit, scale = k.logit_unit[...], k.logit_scale[:, :1]
    weighted = upstream * k.head_gain[0:1]
    mean = jnp.sum(weighted, axis=-1, keepdims=True) / s.classes
    along = jnp.sum(weighted * unit, axis=-1, keepdims=True) / s.classes
    head_row = jnp.sum(upstream * unit, axis=0, keepdims=True)
    d_logits = scale * (weighted - mean - unit * along)
    d_logits = jnp.where(lane_iota(s.own, s.lanes) < s.classes, d_logits, 0.0).astype(BF16)
    d_class = transposed_times(d_logits, k.patch_unit[WP : WP + s.own])
    for n in range(4):
        k.class_out[n] = jnp.concatenate(
            [d_class[s.step * n : s.step * (n + 1)], jnp.zeros((s.slot - s.step, s.dim), F32)], axis=0
        ).astype(BF16)
    for slot in (k.ts, k.tx, k.td):
        net.send(k.class_out.at[slot], k.class_in.at[t], k.at.class_, t, (i, slot))
    final = k.final[...]
    c = lax.rsqrt(jnp.sum(final * final, axis=-1, keepdims=True) + 1e-06)
    u = final * c

    def unit_back(rows, du):
        return c[rows] * (du - u[rows] * jnp.sum(u[rows] * du, axis=-1, keepdims=True))

    d_patch = unit_back(slice(0, s.own), product(d_logits, k.class_unit[...]))
    k.d_rows[: s.own] = d_patch
    k.d_branch[t, : s.own] = d_patch.astype(BF16)
    share_start(k, k.d_branch, k.at.d_branch, patch_part)
    d_class_unit = k.class_out[t].astype(F32)
    for slot in (k.ts, k.tx, k.td):
        net.arrived(k.class_in.at[slot], k.at.class_, slot)
        d_class_unit = d_class_unit + k.class_in[slot].astype(F32)
    d_class = unit_back(slice(s.own, s.rows), d_class_unit)
    k.d_rows[s.own :] = d_class
    k.d_branch[t, s.own :] = d_class.astype(BF16)
    share_start(k, k.d_branch, k.at.d_class, class_part)

    def feed_back(slot):
        d_act = times_transposed(k.d_branch[slot], k.w_reduce[...].reshape(s.hidden, s.dim))
        d_pre = (d_act * k.slope[slot].astype(F32)).astype(BF16)
        k.d_pre[slot] = d_pre
        return times_transposed(d_pre, k.w_expand[...].reshape(s.dim, s.hidden))

    def ready(slot):
        if slot is k.tx:
            share_pass(k, k.d_branch, k.at.d_branch, patch_part)
            share_pass(k, k.d_branch, k.at.d_class, class_part)
        else:
            net.arrived(k.d_branch.at[slot, patch_part], k.at.d_branch, slot)
            net.arrived(k.d_branch.at[slot, class_part], k.at.d_class, slot)

    reduce_over_tile(k, k.at.feed, feed_back, ready)
    tall = 4 * s.rows
    put_blocks(
        k,
        BACK,
        transposed_times(k.act[...].reshape(tall, s.hidden), k.d_branch[...].reshape(tall, s.dim)),
    )
    if comm:
        sum_start(k, BACK)
    put_blocks(
        k,
        INTO,
        transposed_times(k.h_two[...].reshape(tall, s.dim), k.d_pre[...].reshape(tall, s.hidden)),
    )
    if comm:
        sum_start(k, INTO)

    unit, scale = layer_norm_parts(k.after[...])
    part, gain_two_row = layer_norm_back(unit, scale, k.gains[1:2], reduced_over_tile(k, k.at.feed))
    d_after = k.d_rows[...] + part
    k.d_rows[...] = d_after
    d_attn = d_after.astype(BF16)
    k.d_attn[t] = d_attn
    wide = s.here * s.head
    w_project = k.w_project[...].reshape(s.dim, s.dim)
    for n in range(4):
        k.d_mixed_out[n] = times_transposed(d_attn, w_project[wide * n : wide * (n + 1)]).astype(BF16)
    k.d_mixed[t] = k.d_mixed_out[t]
    for slot in (k.tx, k.td, k.ts):
        net.send(k.d_mixed_out.at[slot], k.d_mixed.at[t], k.at.d_mixed, t, (i, slot))
    share_start(k, k.d_attn, k.at.d_attn)
    if comm:
        sum_pass(k, BACK)

    for h in range(s.here):

        def block(slot):
            rows = slot_rows(k, slot)
            out = k.outs[h, rows, :]
            inverse = 1.0 / out[:, s.head : s.head + 1]
            largest = out[:, s.head + 1 : s.head + 2]
            powers = jnp.exp(block_scores(k, h, slot) - largest).astype(BF16)
            k.powers[rows, :] = powers
            d_mixed = k.d_mixed[slot][:, s.head * h : s.head * (h + 1)].astype(F32)
            scaled = (d_mixed * inverse).astype(BF16).astype(F32)
            along = jnp.sum(scaled * out[:, : s.head], axis=-1, keepdims=True) * inverse
            high = along.astype(BF16).astype(F32)
            lane = lane_iota(s.rows, s.head)
            tail = jnp.where(lane == 0, -high, jnp.where(lane == 1, high - along, 0.0))
            left = jnp.concatenate([scaled, tail], axis=1).astype(BF16)
            k.d_out[rows, :] = left
            d_scores = (powers.astype(F32) * times_transposed(left, k.values[h])).astype(BF16)
            k.d_scores[rows, :] = d_scores
            k.d_q[rows, :] = product(d_scores, k.keys[h])

        for slot in (t, k.ts, k.tx, k.td):
            if h == 0 and slot is not t:
                net.arrived(k.d_mixed.at[slot], k.at.d_mixed, slot)
            block(slot)
        d_k = transposed_times(k.q[h][:, : s.head], k.d_scores[...])
        d_v = transposed_times(k.d_out[:, : s.head], k.powers[...])
        k.d_joint[h] = jnp.concatenate(
            [k.d_q[:, : s.head] * s.head**-0.5, d_k.T, d_v.T], axis=1
        ).astype(BF16)
        put_blocks(
            k,
            JOINT + h,
            transposed_times(k.h_one[...].reshape(tall, s.dim), k.d_joint[h]),
        )
        if comm:
            sum_start(k, JOINT + h)
        if h == 0:
            share_pass(k, k.d_attn, k.at.d_attn)
            if comm:
                sum_pass(k, INTO)
        if h == 1:
            net.arrived(k.d_attn.at[k.ts], k.at.d_attn, k.ts)
            net.arrived(k.d_attn.at[k.td], k.at.d_attn, k.td)
            d_project = transposed_times(
                k.mixed[...].reshape(tall, wide), k.d_attn[...].reshape(tall, s.dim)
            )
            if comm:
                shard = s.dim // s.images
                for y in range(PLANE):
                    k.project_out[y] = d_project[shard * y : shard * (y + 1)].astype(BF16)
                net.send(k.project_out.at[1 - k.y], k.project_mate, k.at.project_mate, 0, k.mate)
                sum_pass(k, JOINT)
                sum_end(k, BACK)
            else:
                k.d_project[...] = d_project.astype(BF16)

    w_joint = k.w_joint[...].reshape(s.dim, 3 * wide)

    def joint_back(slot):
        rows = slot_rows(k, slot)
        left = jnp.concatenate([k.d_joint[h, rows, :] for h in range(s.here)], axis=1)
        return times_transposed(left, w_joint)

    reduce_over_tile(k, k.at.joint, joint_back, lambda slot: None)

    if comm:
        sum_pass(k, JOINT + 1)
        sum_end(k, INTO)
        sum_share(k, BACK)
        sum_pass_project(k)
        sum_pass(k, JOINT + 2)
        sum_end(k, JOINT)

    unit, scale = layer_norm_parts(k.token_rows[...])
    part, gain_one_row = layer_norm_back(unit, scale, k.gains[0:1], reduced_over_tile(k, k.at.joint))
    d_tokens = k.d_rows[...] + part
    k.patch_grad[0] = d_tokens[: s.own]

    rows = row_iota(s.slot, s.dim)
    table = jnp.where(rows < s.step, d_tokens[s.own :], 0.0)
    table = jnp.where(rows == s.step, gain_one_row, table)
    table = jnp.where(rows == s.step + 1, gain_two_row, table)
    rows = row_iota(s.slot, 128)
    head_rows = jnp.where(rows == s.step + 2, head_row[:, :128], 0.0)
    rest = jnp.concatenate(
        [head_row[:, 128:], jnp.zeros((1, 256 - s.lanes), F32)], axis=1
    )
    head_rows = jnp.where(rows == s.step + 3, rest, head_rows)
    if not comm:
        k.small_out[...] = table
        k.head_out[...] = head_rows
        net.drain()
        return
    pad = jnp.zeros((s.slot, 128 - shard), F32)
    for n in range(s.images):
        cut = table[:, shard * n : shard * (n + 1)]
        k.small_out[n] = jnp.concatenate([cut, pad], axis=1) + head_rows
    for step in range(1, s.images):
        n = (i + step) % s.images
        net.send(k.small_out.at[n], k.small_in.at[i], k.at.small, i, (n, t))
    sum_share(k, INTO)
    total = k.small_out[i]
    for step in range(1, s.images):
        n = (i + step) % s.images
        net.arrived(k.small_in.at[n], k.at.small, n)
        total = total + k.small_in[n]
    k.small_sum[t] = total
    for slot in (k.ts, k.tx, k.td):
        net.send(k.small_sum.at[t], k.small_sum.at[t], k.at.small_sum, t, (i, slot))
    sum_end(k, JOINT + 1)
    sum_end_project(k)
    sum_end(k, JOINT + 2)
    for h in range(s.here):
        sum_share(k, JOINT + h)
    write_gradients(k)
    net.drain()


def write_gradients(k):
    s = k.s
    shard = s.dim // s.images
    for name in range(len(k.grads)):
        sum_close(k, name)
    for n in range(4):
        k.d_w_back[shard * n : shard * (n + 1)] = k.grads[BACK].out[n].astype(F32)
    part = s.hidden // s.images
    cut = [k.grads[INTO].out[n].astype(F32) for n in range(4)]
    cut = [cut[n][:, part * i : part * (i + 1)] for i in range(s.images) for n in range(4)]
    k.d_w_in[...] = jnp.concatenate(cut, axis=1)
    for m in range(3):
        cut = [
            k.grads[JOINT + h].out[n].astype(F32)[:, s.head * m : s.head * (m + 1)]
            for n in range(4)
            for h in range(s.here)
        ]
        k.d_w_qkv[:, s.dim * m : s.dim * (m + 1)] = jnp.concatenate(cut, axis=1)
    k.d_w_out[...] = k.d_project[...].astype(F32)
    for slot in (k.ts, k.tx, k.td):
        k.net.arrived(k.small_sum.at[slot], k.at.small_sum, slot)
    rows = jnp.concatenate([k.small_sum[n][: s.step] for n in range(4)], axis=0)
    k.d_cls[...] = rows[: s.classes, :shard]
    rest = k.small_sum[0] + k.small_sum[1] + k.small_sum[2] + k.small_sum[3]
    k.d_gains[...] = rest[s.step : s.step + 8]


def sum_pass_project(k):
    net = k.net
    net.arrived(k.project_mate, k.at.project_mate, 0)
    both = k.project_out[k.y].astype(F32) + k.project_mate[...].astype(F32)
    k.project_both[...] = both.astype(BF16)
    net.send(
        k.project_both, k.project_line.at[k.z], k.at.project_line, k.z, (PLANE * k.t + k.y, k.t), k.z != k.t
    )


def sum_end_project(k):
    net = k.net
    mine = k.z == k.t

    @pl.when(mine)
    def _():
        total = k.project_both[...].astype(F32)
        for step in range(1, k.planes):
            z = (k.z + step) % k.planes
            net.arrived(k.project_line.at[z], k.at.project_line, z)
            total = total + k.project_line[z].astype(F32)
        k.d_project[...] = total.astype(BF16)

    for step in range(1, 4):
        slot = (k.t + step) % 4
        net.send(k.d_project, k.d_project, k.at.project, 0, (k.i, slot), mine)

    @pl.when(jnp.logical_not(mine))
    def _():
        net.arrived(k.d_project, k.at.project, 0)


def tent(pixels, cells, first):
    place = (np.arange(pixels) + 0.5) / UP - 0.5 - first
    return np.maximum(0.0, 1.0 - np.abs(place[:, None] - np.arange(cells)[None, :]))


def band_tables():
    across = (np.clip((np.arange(WP * UP) + 0.5) / UP - 0.5, 0, WP - 1))[None, :]
    across = np.maximum(0.0, 1.0 - np.abs(across - np.arange(WP)[:, None]))
    down = tent(BAND, BAND_CELLS, -1)
    up = np.zeros((GROUP, BAND, 2, BAND_CELLS, GROUP), np.float32)
    back = np.zeros((BAND_CELLS, GROUP, GROUP, BAND), np.float32)
    for c in range(GROUP):
        up[c, :, :, :, c] = down[:, None, :]
        back[:, c, c, :] = down.T
    up = up.reshape(GROUP * BAND, 2 * BAND_CELLS * GROUP)
    back = back.reshape(BAND_CELLS * GROUP, GROUP * BAND)
    return [jnp.asarray(t, BF16) for t in (across, up, back)]


def two_parts(value):
    high = value.astype(BF16)
    return high, (value - high.astype(F32)).astype(BF16)


def upsample_kernel(
    classes, bands, height_ref, cell_ref, label_ref, across_ref, up_ref, back_ref, mask_ref, sum_ref,
    wide, wide_grad, powers,
):
    band = pl.program_id(0)
    groups = -(-classes // GROUP)
    tail = classes - GROUP * (groups - 1)
    rows = cell_ref.shape[0] // WP
    pixels = label_ref.shape[2]

    @pl.when(band == 0)
    def _():
        for r in range(rows):
            wide[r] = lax.dot_general(
                cell_ref[WP * r : WP * (r + 1), :], across_ref[...], (((0,), (0,)), ((), ())),
                preferred_element_type=F32,
            )
        wide_grad[...] = jnp.zeros_like(wide_grad)

    step = BAND // UP

    def forward(g, total, count):
        part = wide[pl.ds(step * band, BAND_CELLS), pl.ds(GROUP * g, GROUP), :]
        both = jnp.concatenate(two_parts(part.reshape(BAND_CELLS * GROUP, pixels)), axis=0)
        upsampled = product(up_ref[: count * BAND, :], both).reshape(count, BAND, pixels)
        mask_ref[pl.ds(GROUP * g, count)] = upsampled.astype(BF16)
        power = jnp.exp(upsampled)
        powers[pl.ds(GROUP * g, count)] = power
        return total + jnp.sum(power, axis=0)

    total = jnp.zeros((BAND, pixels), F32)
    for g in range(groups):
        total = forward(g, total, GROUP if g < groups - 1 else tail)
    pixel_rows = lax.broadcasted_iota(jnp.int32, (BAND, pixels), 0) + BAND * band
    limit = (height_ref[0] - lax.axis_index(TILE) * (bands * BAND // UP)) * UP
    label = jnp.where(pixel_rows < limit, label_ref[0], -1)
    share = 1.0 / (UP * UP)
    inverse = jnp.where(label >= 0, share, 0.0) / total

    def backward(g, count):
        parts = []
        for c in range(count):
            target = jnp.where(label == GROUP * g + c, share, 0.0)
            parts.append((powers[GROUP * g + c] * inverse - target).astype(BF16))
        summed = product(back_ref[:, : count * BAND], jnp.concatenate(parts, axis=0))
        wide_grad[pl.ds(step * band, BAND_CELLS), pl.ds(GROUP * g, GROUP), :] += summed.reshape(
            BAND_CELLS, GROUP, pixels
        )

    for g in range(groups):
        backward(g, GROUP if g < groups - 1 else tail)

    @pl.when(band == bands - 1)
    def _():
        for r in range(rows):
            high, low = two_parts(wide_grad[r])
            sum_ref[WP * r : WP * (r + 1), :] = times_transposed(
                across_ref[...], high
            ) + times_transposed(across_ref[...], low)


def upsampled_loss(cells, labels, heights, classes):
    rows, lanes = cells.shape[0] // WP, cells.shape[1]
    tile_pixels, wide_pixels = labels.shape[1:]
    tables = band_tables()
    bands = tile_pixels // BAND

    def whole(shape):
        return pl.BlockSpec(shape, lambda i: (0,) * len(shape))

    return pl.pallas_call(
        functools.partial(upsample_kernel, classes, bands),
        grid=(bands,),
        out_shape=(
            jax.ShapeDtypeStruct((classes, tile_pixels, wide_pixels), BF16),
            jax.ShapeDtypeStruct(cells.shape, F32),
        ),
        in_specs=[
            pl.BlockSpec(memory_space=pltpu.SMEM),
            whole(cells.shape),
            pl.BlockSpec((1, BAND, wide_pixels), lambda i: (0, i, 0)),
        ]
        + [whole(t.shape) for t in tables],
        out_specs=(
            pl.BlockSpec((classes, BAND, wide_pixels), lambda i: (0, i, 0)),
            whole(cells.shape),
        ),
        scratch_shapes=[
            pltpu.VMEM((rows, lanes, wide_pixels), F32),
            pltpu.VMEM((rows, lanes, wide_pixels), F32),
            pltpu.VMEM((lanes, BAND, wide_pixels), F32),
        ],
        compiler_params=pltpu.CompilerParams(vmem_limit_bytes=56 << 20),
        name=upsample_kernel.__name__,
    )(heights, cells, labels, *tables)


CELLS = "cells"
GRAD_REFS = ("out", "blocks", "from_mate", "both", "from_line")
GRAD_PLACES = ("at_mate", "at_line", "at_out")
Grad = collections.namedtuple("Grad", GRAD_REFS + GRAD_PLACES)


def run_kernel(body, s, inputs, outputs, scratch, recv, sends, number):
    names_in, names_out, names_scratch = list(inputs), list(outputs), list(scratch)

    places = types.SimpleNamespace()
    arrivals = 0
    for name, count in recv.items():
        setattr(places, name, arrivals)
        arrivals += count

    def kernel(*refs):
        k = types.SimpleNamespace(s=s, at=places)
        for name, ref in zip(names_in + names_out + names_scratch, refs):
            setattr(k, name, ref)
        k.send_sem, k.recv_sem = refs[-2:]
        k.net = Net(k)
        k.grads = []
        for n in range(JOINT + s.here):
            of = [getattr(k, word + str(n), None) for word in GRAD_REFS]
            at = [getattr(places, word + str(n), None) for word in GRAD_PLACES]
            k.grads.append(Grad(*of, *at))
        body(k)

    def space(name):
        scalar = name in inputs and inputs[name].ndim == 1
        return pl.BlockSpec(memory_space=pltpu.SMEM if scalar else pltpu.VMEM)

    results = pl.pallas_call(
        kernel,
        out_shape=[jax.ShapeDtypeStruct(*outputs[n]) for n in names_out],
        in_specs=[space(n) for n in names_in],
        out_specs=[space(n) for n in names_out],
        scratch_shapes=[pltpu.VMEM(*scratch[n]) for n in names_scratch]
        + [pltpu.SemaphoreType.DMA((sends,)), pltpu.SemaphoreType.DMA((arrivals,))],
        compiler_params=pltpu.CompilerParams(
            collective_id=number, has_side_effects=True, vmem_limit_bytes=VMEM_BYTES
        ),
        name=body.__name__,
    )(*inputs.values())
    return dict(zip(names_out, results))


def reduce_scratch(s):
    return dict(
        stage=((3, s.rows, s.dim), BF16),
        from_sib=((2, s.rows, s.dim), BF16),
        from_across=((s.rows, s.dim), BF16),
        own_part=((s.rows, s.dim), F32),
        across_part=((s.rows, s.dim), F32),
    )


def forward_call(s, inputs):
    wide = s.here * s.head
    all_rows = 4 * s.rows
    outputs = dict(
        h_one=((4, s.rows, s.dim), BF16),
        q=((s.here, all_rows, 2 * s.head), BF16),
        keys=((s.here, all_rows, 2 * s.head), BF16),
        values=((s.here, all_rows, 2 * s.head), BF16),
        outs=((s.here, all_rows, 2 * s.head), F32),
        mixed=((4, s.rows, wide), BF16),
        token_rows=((s.rows, s.dim), F32),
        after=((s.rows, s.dim), F32),
        h_two=((4, s.rows, s.dim), BF16),
        act=((4, s.rows, s.hidden), BF16),
        slope=((4, s.rows, s.hidden), BF16),
        final=((s.rows, s.dim), F32),
        patch_unit=((s.own + 2 * WP, s.dim), BF16),
        head_gain=((8, s.lanes), F32),
        class_unit=((s.lanes, s.dim), BF16),
        logit_unit=((s.own, s.lanes), F32),
        logit_scale=((s.own, 128), F32),
        cells=((s.own + 2 * WP, s.lanes), BF16),
        gains=((8, s.dim), F32),
    )
    scratch = dict(
        tokens=((4, s.own, s.dim), BF16),
        cls_rows=((s.lanes, s.dim), F32),
        mixed_all=((4, s.rows, wide), BF16),
        cls_units=((4, s.slot, s.dim), BF16),
        **reduce_scratch(s),
    )
    recv = dict(tokens=4, mixed=4, h_two=4, feed=3, units=4, rim=2)
    sends = 3 + 3 + 3 + 3 + 3 + 2
    if s.img_comm:
        shard = s.dim // s.images
        outputs.update(w_joint=((s.images, shard, 3 * wide), BF16))
        outputs.update(w_project=((4, PLANE, shard, s.dim), BF16))
        scratch.update(small=((s.lanes, 128), BF16), wq=((shard, 3 * wide), BF16))
        scratch.update(wi=((shard, s.hidden), BF16))
        outputs.update(w_expand=((s.images, shard, s.hidden), BF16))
        outputs.update(w_reduce=((s.images, shard, s.dim), BF16))
        scratch.update(smalls=((s.images, s.lanes, 128), BF16))
        n = s.images
        recv.update(small=n, w_joint=n, w_project=2, w_shared=4, w_expand=n, w_reduce=n)
        sends += 4 * (2 * (n // PLANE) - 1) + n // PLANE + 3
    return run_kernel(forward_kernel, s, inputs, outputs, scratch, recv, sends, 1)


def backward_call(s, inputs):
    wide = s.here * s.head
    all_rows = 4 * s.rows
    outputs = dict(patch_grad=((1, s.own, s.dim), F32))
    scratch = dict(
        rim_in=((2, WP, s.lanes), F32),
        class_out=((4, s.slot, s.dim), BF16),
        class_in=((4, s.slot, s.dim), BF16),
        d_rows=((s.rows, s.dim), F32),
        d_branch=((4, s.rows, s.dim), BF16),
        d_pre=((4, s.rows, s.hidden), BF16),
        d_attn=((4, s.rows, s.dim), BF16),
        d_mixed_out=((4, s.rows, wide), BF16),
        d_mixed=((4, s.rows, wide), BF16),
        powers=((all_rows, all_rows), BF16),
        d_scores=((all_rows, all_rows), BF16),
        d_out=((all_rows, 2 * s.head), BF16),
        d_q=((all_rows, 2 * s.head), F32),
        d_joint=((s.here, all_rows, 3 * s.head), BF16),
        **reduce_scratch(s),
    )
    recv = dict(rim=2, class_=4, d_branch=4, d_class=4, feed=3, d_mixed=4, d_attn=4, joint=3)
    sends = 2 + 3 + 3 + 3 + 3 + 3 + 3 + 3
    columns = [s.dim, s.hidden] + [3 * s.head] * s.here
    planes, shard = s.images // PLANE, s.dim // s.images
    for n, cols in enumerate(columns):
        out, blocks, from_mate, both, from_line = [word + str(n) for word in GRAD_REFS]
        at_mate, at_line, at_out = [word + str(n) for word in GRAD_PLACES]
        if not s.img_comm:
            outputs[out] = ((s.dim, cols), BF16)
            continue
        scratch[out] = ((4, shard, cols), BF16)
        scratch[blocks] = ((PLANE, planes, shard, cols), BF16)
        for what in (from_mate, both, from_line):
            scratch[what] = ((planes, shard, cols), BF16)
        recv[at_mate] = 1
        recv[at_line] = planes
        recv[at_out] = 4
        sends += 1 + planes - 1 + 3
    if s.img_comm:
        outputs.update(d_w_back=((4 * shard, s.dim), F32))
        outputs.update(d_w_in=((shard, 4 * s.hidden), F32))
        outputs.update(d_w_qkv=((shard, 12 * wide), F32))
        outputs.update(d_w_out=((shard, s.dim), F32))
        outputs.update(d_cls=((s.classes, shard), F32))
        outputs.update(d_gains=((8, 128), F32))
        scratch.update(d_project=((shard, s.dim), BF16))
        scratch.update(small_sum=((4, s.slot, 128), F32))
        scratch.update(project_out=((PLANE, shard, s.dim), BF16))
        scratch.update(project_mate=((shard, s.dim), BF16))
        scratch.update(project_both=((shard, s.dim), BF16))
        scratch.update(project_line=((planes, shard, s.dim), BF16))
        scratch.update(small_out=((s.images, s.slot, 128), F32))
        scratch.update(small_in=((s.images, s.slot, 128), F32))
        recv.update(project_mate=1, project_line=planes, project=1, small=s.images, small_sum=4)
        sends += 1 + 1 + 3 + s.images - 1 + 3
    else:
        outputs.update(d_project=((wide, s.dim), BF16))
        outputs.update(small_out=((s.slot, s.dim), F32))
        outputs.update(head_out=((s.slot, 128), F32))
    return run_kernel(backward_kernel, s, inputs, outputs, scratch, recv, sends, 2)


def sizes(patches, cls_emb, w_joint, w_back, head_gain):
    images, tiles = lax.axis_size(IMG), lax.axis_size(TILE)
    s = types.SimpleNamespace(images=images, tiles=tiles)
    s.dim = patches.shape[2]
    s.own = patches.shape[1]
    s.grid = s.own // WP
    s.classes = head_gain.shape[0]
    s.step = -(-s.classes // (8 * tiles)) * 8
    s.slot = -(-s.step // 16) * 16
    s.lanes = s.step * tiles
    s.rows = s.own + s.slot
    s.head = s.dim // HEADS
    s.here = HEADS // tiles
    s.hidden = w_back.shape[0] * images // tiles
    shard = w_joint.shape[0]
    s.img_comm = images == PLANE * tiles and shard % 16 == 0 and shard <= 128
    return s


def shards(
    patches, labels, heights, cls_emb, gain_one, w_qkv, w_out, gain_two, w_in, w_back, head_gain
):
    s = sizes(patches, cls_emb, w_qkv, w_back, head_gain)
    t = lax.axis_index(TILE)
    shard = w_qkv.shape[0]
    wide = s.here * s.head

    part = w_back.shape[0] // s.tiles
    w_back = w_back.reshape(s.tiles, part, s.dim)
    cls_emb, gain_one, gain_two = cls_emb, gain_one[None], gain_two[None]
    inputs = dict(patches=patches, height=heights, gain_row=head_gain[None])
    common = {}
    if s.img_comm:
        inputs.update(cls_emb=cls_emb, gain_one=gain_one, gain_two=gain_two)
        inputs.update(w_qkv=w_qkv, wo=w_out, w_in=w_in, wb=w_back)
    else:

        def gather(value, axis=0):
            return lax.all_gather(value, IMG, axis=axis, tiled=True)

        def pick(value, axis):
            return lax.dynamic_index_in_dim(value, t, axis, keepdims=False)

        joint = pick(w_qkv.reshape(shard, 3, s.tiles, s.here, s.head), 2)
        joint = joint.transpose(0, 2, 1, 3).reshape(shard, 3 * wide)
        expand = pick(w_in.reshape(shard, s.images, s.tiles, part), 2).reshape(shard, s.hidden)
        reduce = pick(w_back, 0)
        small = jnp.concatenate([cls_emb, gain_one, gain_two], axis=0)
        small = jnp.pad(small, ((0, s.lanes - small.shape[0]), (0, 0)))
        common.update(
            w_joint=gather(joint)[None],
            w_project=gather(w_out)[None],
            w_expand=gather(expand)[None],
            w_reduce=gather(reduce)[None],
        )
        inputs.update(small_full=gather(small, 1), **common)
    kept = forward_call(s, inputs)
    cells = kept.pop(CELLS)
    masks, cell_sums = upsampled_loss(cells, labels, heights, s.classes)
    grads = backward_call(s, dict(**kept, **common, cell_sums=cell_sums))
    grads = types.SimpleNamespace(**grads)
    if s.img_comm:
        head_grad = grads.d_gains[2:4].reshape(-1)[: s.classes]
        return (
            masks[None],
            grads.patch_grad,
            grads.d_cls,
            grads.d_gains[0, :shard],
            grads.d_w_qkv,
            grads.d_w_out,
            grads.d_gains[1, :shard],
            grads.d_w_in,
            grads.d_w_back,
            head_grad,
        )

    def across(value):
        return lax.all_gather(value, TILE, axis=0, tiled=False)

    def total(value, axis=0):
        return lax.psum_scatter(value, IMG, scatter_dimension=axis, tiled=True)

    pieces = [getattr(grads, GRAD_REFS[0] + str(n)) for n in range(JOINT + s.here)]
    pieces = [across(total(v)) for v in pieces]
    project = total(lax.all_gather(grads.d_project, TILE, axis=0, tiled=True))
    small = across(total(grads.small_out, 1))
    head_rows = across(lax.psum(grads.head_out, IMG))
    joint = jnp.stack(pieces[JOINT:], axis=0)
    joint = joint.reshape(s.here, s.tiles, shard, 3, s.head).transpose(2, 3, 1, 0, 4)
    expand = pieces[INTO].reshape(s.tiles, shard, s.images, part).transpose(1, 2, 0, 3)
    cls_grad = small[:, : s.step, :shard].reshape(s.lanes, shard)[: s.classes]
    gain_grads = jnp.sum(small[:, s.step : s.step + 2, :shard], axis=0)
    head_grad = jnp.sum(head_rows[:, s.step + 2 : s.step + 4, :128], axis=0).reshape(-1)[: s.classes]
    return (
        masks[None],
        grads.patch_grad,
        cls_grad,
        gain_grads[0],
        joint.reshape(shard, -1).astype(F32),
        project.astype(F32),
        gain_grads[1],
        expand.reshape(shard, -1).astype(F32),
        pieces[BACK].reshape(-1, s.dim).astype(F32),
        head_grad,
    )


def solution(mesh):
    in_specs = (
        P(IMG, TILE, None),
        P(IMG, TILE, None),
        P(IMG),
        P(None, IMG),
        P(IMG),
        P(IMG, None),
        P(IMG, None),
        P(IMG),
        P(IMG, None),
        P(IMG, None),
        P(),
    )
    out_specs = (
        P(IMG, None, TILE, None),
        P(IMG, TILE, None),
        P(None, IMG),
        P(IMG),
        P(IMG, None),
        P(IMG, None),
        P(IMG),
        P(IMG, None),
        P(IMG, None),
        P(),
    )
    return jax.shard_map(shards, mesh=mesh, in_specs=in_specs, out_specs=out_specs, check_vma=False)
```

time: 1210 us -> 249 us (0.21)
  waiting for transfers between devices: 808 us -> 0 us
  Pallas kernels: 18.1 us -> 234 us
  blocking collectives: 146 us -> 0 us
  matrix products: 112 us -> 0 us
  other arithmetic: 40 us -> 0 us
  local copies, waits for them, and re-layouts: 35.4 us -> 10.8 us
  starting transfers between devices: 22 us -> 0 us
  between operations: 18.6 us -> 1.56 us
    reduce_scatter x4 -> x0, waiting for transfers between devices: 499 us -> none  [the longest x1 164 us: shards(): lax.psum_scatter(w_back_grad, 'img', scatter_dimension=0, tiled=True)]
    pallas_call x0 -> x2, Pallas kernels: none -> 216 us  [run_kernel(): pl.pallas_call(kernel, out_shape=[jax.ShapeDtypeStruct(*outputs[n]) for n...]
    all_gather x5 -> x0, waiting for transfers between devices: 198 us -> none  [the longest x1 78.3 us: shards(): lax.all_gather(w_in, 'img', axis=0, tiled=True)]
    dot_general x20 -> x0, matrix products: 102 us -> none  [the longest x5 24.7 us: transposed_times(): lax.dot_general(left, right, (((0,), (0,)), ((), ())), preferred_element_...]
    unnamed x15 -> x0, waiting for transfers between devices: 73.2 us -> none
    unnamed x3 -> x0, blocking collectives: 55.7 us -> none
    psum x2 -> x0, blocking collectives: 50.7 us -> none  [the longest x1 39.6 us: shards(): head_total = lax.psum(head_grad, ('img', 'tile'))]
    all_gather x2 -> x0, blocking collectives: 39.6 us -> none  [the longest x1 33.8 us: shards(): lax.all_gather(cls_emb, 'img', axis=1, tiled=True)]
  transfers between devices with their start and end apart: 17 -> 0, of which waited for: 13 -> 0; matrix products, arithmetic and copies ran while one was open for 9% -> 0% of each run, Pallas kernels for 0% -> 0%
where the time goes in v2:
time: 249 us; the launch traced here: 247 us
  Pallas kernels  234 us (94%)
  local copies, waits for them, and re-layouts  10.8 us (4%)
    pallas_call x2, Pallas kernels, run_kernel(): pl.pallas_call(kernel, out_shape=[jax.ShapeDtypeStruct(*outputs[n]) for n...  216 us
    pallas_call x1, Pallas kernels, upsampled_loss(): pl.pallas_call(functools.partial(upsample_kernel, classes, bands), grid=(...  18.2 us
    unnamed x16, local copies, waits for them, and re-layouts  7.05 us

profile of v2, /device:TPU:0, one launch (start us, length us, event | category | flops | bytes accessed | tf_op | source)
XLA Modules:
  0.0 246.7 jit_solution(1472907532907707306)
XLA Ops:
  1.3 1.2 broadcast_in_dim.12.refs_2_
  2.5 95.8 %forward_kernel.1 = (bf16[4,304,768]{2,1,0:T(8,128)(2,1)}, bf16[3,1216,128]{2,1,0:T(8,128)(2,1)}, bf16[3,1216,128]{2,1,0:T(8,128)(2,1)}, bf16[3,1216,128]{2,1,0:...) custom-call(bf16[1,256,768]{2,1,0:T(8,128)(2,1)} %refs_0_.1, ...), custom_call_target="tpu_custom_call" | custom-call | tf_op jit(solution)/shard_map/forward_kernel/pallas_call | solution.py:941
  98.3 18.2 %upsample_kernel.1 = (bf16[150,256,256]{2,1,0:T(8,128)(2,1)}, f32[288,160]{1,0:T(8,128)}) custom-call(s32[1]{0:T(128)S(6)} %copy.30.refs_1_.height_ref, bf16[288,160]{1,0:T(8,128)(2,1)} %get-tuple-element.42.cell_ref, s32[1,256,256]{2,1,0:T(8,128)} %label_ref.1, bf16[16,256]{1,0:T(8,128)(2,1)} %constant.6.clone.across_ref, ...), custom_call_target="tpu_custom_call" | custom-call | tf_op jit(solution)/shard_map/upsample_kernel/pallas_call | solution.py:882
  116.5 120.4 %backward_kernel.1 = (f32[1,256,768]{2,1,0:T(8,128)}, f32[384,768]{1,0:T(8,128)}, f32[96,3072]{1,0:T(8,128)}, f32[96,2304]{1,0:T(8,128)}, f32[96,768]{1,0:T(8,12...) custom-call(bf16[4,304,768]{2,1,0:T(8,128)(2,1)} %get-tuple-element.44.refs_0_, ...), custom_call_target="tpu_custom_call" | custom-call | tf_op jit(solution)/shard_map/backward_kernel/pallas_call | solution.py:941
  236.9 0.0 copy-start.4
  236.9 0.0 copy-start.2
  236.9 1.3 slice_bitcast_fusion.1
  238.2 1.2 slice_bitcast_fusion
  239.4 2.1 copy.31
  241.5 0.0 copy-done.4
  241.5 0.0 copy-start.3
  241.5 0.6 copy.32
  242.1 0.0 copy-done.2
  242.1 0.0 copy-start.1
  242.1 0.9 copy.33
  243.0 0.0 copy-done.3
  243.0 0.7 copy.34
  243.7 0.0 copy-done.1
  243.7 0.0 copy-start
  243.7 1.0 copy.35
  244.8 0.7 copy-done
  245.4 1.0 copy.36
Async XLA Ops:
  236.9 4.6 %copy-start.4 = (f32[150,96]{1,0:T(8,128)S(1)}, f32[150,96]{1,0:T(8,128)}, u32[]{:S(2)}) copy-start(f32[150,96]{1,0:T(8,128)} %get-tuple-element.88) | copy-start | bytes 172804
  236.9 5.2 %copy-start.2 = (f32[96,2304]{1,0:T(8,128)S(1)}, f32[96,2304]{1,0:T(8,128)}, u32[]{:S(2)}) copy-start(f32[96,2304]{1,0:T(8,128)} %get-tuple-element.90) | copy-start | bytes 2654212
  241.5 1.6 copy-start.3
  242.1 1.6 copy-start.1
  243.7 1.7 copy-start
